TPU v7x, 32 devices: a whole 2x2x4 slice. The times are simulated.
32 devices in a mesh: tower: 2 (over x), dp: 16 (over z, y, core).
Axes of the slice: x: 2, y: 2, z: 4, core: 2. Of those that a mesh axis runs over, the one named last changes fastest.
Arguments:
- tokens: bfloat16 [2, 2, 16, 512, 768], P('tower', None, 'dp')
- segments: int32 [2, 2, 16, 512], P('tower', None, 'dp'), may hold values from 0 to 7, never falling along the last dimension, each value on 1 to 256 neighbouring positions
- positives: int32 [2, 128], P(None, 'dp'), may hold values from 0 to 127, each once within a row
- token_grad: float32 [2, 2, 16, 512, 768], P('tower', None, 'dp'), may hold values from -6 to 6
- mix_weight: float32 [2, 768, 2304], P('tower', 'dp'), may hold values from -0.109375 to 0.109375
- out_weight: float32 [2, 768, 768], P('tower', 'dp'), may hold values from -1.75 to 1.75
- up_weight: float32 [2, 768, 3072], P('tower', 'dp'), may hold values from -0.21875 to 0.21875
- down_weight: float32 [2, 3072, 768], P('tower', 'dp'), may hold values from -0.109375 to 0.109375
- vectors: float32 [2, 12, 768], P('tower', None, 'dp')
- first_mix: float32 [2, 768, 2304], P('tower', 'dp'), may hold values from -0.0004272461 to 0.0004272461
- first_out: float32 [2, 768, 768], P('tower', 'dp'), may hold values from -0.0004272461 to 0.0004272461
- first_up: float32 [2, 768, 3072], P('tower', 'dp'), may hold values from -0.0004272461 to 0.0004272461
- first_down: float32 [2, 3072, 768], P('tower', 'dp'), may hold values from -0.0004272461 to 0.0004272461
- first_vectors: float32 [2, 12, 768], P('tower', None, 'dp'), may hold values from -0.00061035156 to 0.00061035156
- second_mix: float32 [2, 768, 2304], P('tower', 'dp'), may hold values from 3.5275338e-11 to 5.644054e-10
- second_out: float32 [2, 768, 768], P('tower', 'dp'), may hold values from 1.4110136e-12 to 7.055068e-12
- second_up: float32 [2, 768, 3072], P('tower', 'dp'), may hold values from 3.5275338e-11 to 5.644054e-10
- second_down: float32 [2, 3072, 768], P('tower', 'dp'), may hold values from 3.5275338e-11 to 5.644054e-10
- second_vectors: float32 [2, 12, 768], P('tower', None, 'dp'), may hold values from 1.4110135e-10 to 7.0550676e-10
Outputs:
- layer_output: bfloat16 [2, 2, 16, 512, 768], P('tower', None, 'dp')
- input_grad: float32 [2, 2, 16, 512, 768], P('tower', None, 'dp')
- new_mix: float32 [2, 768, 2304], P('tower', 'dp')
- new_out: float32 [2, 768, 768], P('tower', 'dp')
- new_up: float32 [2, 768, 3072], P('tower', 'dp')
- new_down: float32 [2, 3072, 768], P('tower', 'dp')
- new_vectors: float32 [2, 12, 768], P('tower', None, 'dp')
- moment_mix: float32 [2, 768, 2304], P('tower', 'dp')
- moment_out: float32 [2, 768, 768], P('tower', 'dp')
- moment_up: float32 [2, 768, 3072], P('tower', 'dp')
- moment_down: float32 [2, 3072, 768], P('tower', 'dp')
- moment_vectors: float32 [2, 12, 768], P('tower', None, 'dp')
- square_mix: float32 [2, 768, 2304], P('tower', 'dp')
- square_out: float32 [2, 768, 768], P('tower', 'dp')
- square_up: float32 [2, 768, 3072], P('tower', 'dp')
- square_down: float32 [2, 3072, 768], P('tower', 'dp')
- square_vectors: float32 [2, 12, 768], P('tower', None, 'dp')
- grad_square: float32 [], replicated
Inputs may be any that keep to these rules, and one draw needn't show every extreme that they name: `segments`: in each row the segment numbers never fall, every one of 0 to 7 occurs, and one segment holds exactly 256 tokens. `positives`: within each micro-batch every passage is the positive of exactly one query.
All inputs are finite; a program needn't handle non-finite values.
Results may differ from a plain program's by a relative error of at most 0.012.
The roundings to bfloat16 on the way count: a program that leaves them out, or rounds other values in their place, can miss the bound.
Values may be sent and summed in bfloat16 or wider, within the bound.
No kernel may reach another device: no remote copies, remote signals or barrier semaphores. Data moves between devices by JAX's collectives and lax.ppermute only.
A program may use at most 192 MiB of HBM per device.

v0:
```python
from functools import partial

import jax
import jax.numpy as jnp
from jax import lax
from jax.sharding import PartitionSpec as P

D = 768
FF = 3072
H = 12
HD = 64
L = 512
SEGS = 8
MB = 2
STEP = 5


highest = lax.Precision.HIGHEST
norm_eps = 1e-05
attention_scale = 0.125
score_scale = 0.0625
contrast_weight = 16.0
clip_norm = 1.0
beta_first = 0.9
beta_second = 0.999
adam_eps = 1e-08
weight_decay = 0.01
matrix_rate = 0.05
vector_rate = 0.5
masked_score = -1e30


def passed_along(value, axis, by):
    length = lax.axis_size(axis)
    pairs = [(i, i + by) for i in range(length) if 0 <= i + by < length]
    return lax.ppermute(value, axis, pairs)


def plain_dot(first_op, second_op):
    return jnp.dot(first_op, second_op, preferred_element_type=jnp.float32)


def contract_rows(first_op, second_op):
    return lax.dot_general(
        first_op, second_op, (((0,), (0,)), ((), ())), preferred_element_type=jnp.float32
    )


def contract_cols(first_op, second_op):
    return lax.dot_general(
        first_op, second_op, (((1,), (1,)), ((), ())), preferred_element_type=jnp.float32
    )


def layer_stats(values):
    centred = values - jnp.mean(values, axis=-1, keepdims=True)
    inverse = lax.rsqrt(jnp.mean(centred * centred, axis=-1, keepdims=True) + norm_eps)
    return (centred * inverse, inverse)


def norm_back(upstream, normed, inverse, gain_row):
    gained = upstream * gain_row
    return inverse * (
        gained
        - jnp.mean(gained, axis=-1, keepdims=True)
        - normed * jnp.mean(gained * normed, axis=-1, keepdims=True)
    )


def cls_table(seg_row):
    starts = jnp.sum(
        (seg_row[None, :] < jnp.arange(SEGS, dtype=jnp.int32)[:, None]).astype(jnp.int32), axis=1
    )
    return (jnp.arange(L, dtype=jnp.int32)[None, :] == starts[:, None]).astype(jnp.float32)


def head_split(mixed_low):
    shaped = mixed_low.reshape(L, 3, H, HD)
    return (shaped[:, 0], shaped[:, 1], shaped[:, 2])


def attention_scores(queries, key_rows, seg_row):
    scores = (
        jnp.einsum("qhd,khd->hqk", queries, key_rows, preferred_element_type=jnp.float32)
        * attention_scale
    )
    same_doc = seg_row[:, None] == seg_row[None, :]
    return jnp.where(same_doc[None], scores, masked_score)


def row_forward(params, row_input, seg_row):
    mix_w, out_w, up_w, down_w, vec_f = params
    input_low = row_input.astype(jnp.bfloat16)
    mixed_bias = jnp.concatenate([vec_f[0], jnp.zeros_like(vec_f[0]), vec_f[1]])
    mixed_low = (plain_dot(input_low, mix_w) + mixed_bias).astype(jnp.bfloat16)
    queries, key_rows, value_rows = head_split(mixed_low)
    scores = attention_scores(queries, key_rows, seg_row)
    largest = jnp.max(scores, axis=-1, keepdims=True)
    expo = jnp.exp(scores - largest)
    summed = jnp.sum(expo, axis=-1, keepdims=True)
    probs = expo / summed
    log_total = (largest + jnp.log(summed))[..., 0]
    context = jnp.einsum(
        "hqk,khd->qhd", probs.astype(jnp.bfloat16), value_rows, preferred_element_type=jnp.float32
    )
    context_low = context.reshape(L, D).astype(jnp.bfloat16)
    branch = plain_dot(context_low, out_w) + vec_f[2]
    normed_one, inverse_one = layer_stats(row_input + branch)
    hidden = normed_one * vec_f[3] + vec_f[4]
    hidden_low = hidden.astype(jnp.bfloat16)
    pre_act = plain_dot(hidden_low, up_w) + vec_f[5:9].reshape(FF)
    active_low = jax.nn.gelu(pre_act, approximate=False).astype(jnp.bfloat16)
    ffn_out = plain_dot(active_low, down_w) + vec_f[9]
    normed_two, inverse_two = layer_stats(hidden + ffn_out)
    output = normed_two * vec_f[10] + vec_f[11]
    kept = (
        mixed_low,
        log_total,
        context_low,
        normed_one,
        inverse_one,
        hidden_low,
        pre_act,
        active_low,
        normed_two,
        inverse_two,
    )
    return (output, kept)


def row_backward(params, row_input, seg_row, kept, upstream):
    mix_w, out_w, up_w, down_w, vec_f = params
    (
        mixed_low,
        log_total,
        context_low,
        normed_one,
        inverse_one,
        hidden_low,
        pre_act,
        active_low,
        normed_two,
        inverse_two,
    ) = kept
    gain_two = jnp.sum(upstream * normed_two, axis=0)
    shift_two = jnp.sum(upstream, axis=0)
    grad_pre_two = norm_back(upstream, normed_two, inverse_two, vec_f[10])
    grad_ffn_low = grad_pre_two.astype(jnp.bfloat16)
    bias_down = jnp.sum(grad_ffn_low.astype(jnp.float32), axis=0)
    grad_down = contract_rows(active_low, grad_ffn_low)
    grad_active = contract_cols(grad_ffn_low, down_w)
    gelu_pull = jax.vjp(partial(jax.nn.gelu, approximate=False), pre_act)[1]
    grad_pre_low = gelu_pull(grad_active)[0].astype(jnp.bfloat16)
    bias_up = jnp.sum(grad_pre_low.astype(jnp.float32), axis=0)
    grad_up = contract_rows(hidden_low, grad_pre_low)
    grad_hidden = grad_pre_two + contract_cols(grad_pre_low, up_w)
    gain_one = jnp.sum(grad_hidden * normed_one, axis=0)
    shift_one = jnp.sum(grad_hidden, axis=0)
    grad_pre_one = norm_back(grad_hidden, normed_one, inverse_one, vec_f[3])
    grad_branch_low = grad_pre_one.astype(jnp.bfloat16)
    bias_out = jnp.sum(grad_branch_low.astype(jnp.float32), axis=0)
    grad_out = contract_rows(context_low, grad_branch_low)
    grad_context = contract_cols(grad_branch_low, out_w).astype(jnp.bfloat16).reshape(L, H, HD)
    queries, key_rows, value_rows = head_split(mixed_low)
    scores = attention_scores(queries, key_rows, seg_row)
    probs = jnp.exp(scores - log_total[..., None])
    grad_values = jnp.einsum(
        "hqk,qhd->khd", probs.astype(jnp.bfloat16), grad_context, preferred_element_type=jnp.float32
    )
    grad_probs = jnp.einsum(
        "qhd,khd->hqk", grad_context, value_rows, preferred_element_type=jnp.float32
    )
    grad_scores = probs * (grad_probs - jnp.sum(probs * grad_probs, axis=-1, keepdims=True))
    grad_scores_low = grad_scores.astype(jnp.bfloat16)
    grad_queries = (
        jnp.einsum("hqk,khd->qhd", grad_scores_low, key_rows, preferred_element_type=jnp.float32)
        * attention_scale
    )
    grad_keys = (
        jnp.einsum("hqk,qhd->khd", grad_scores_low, queries, preferred_element_type=jnp.float32)
        * attention_scale
    )
    grad_mixed_low = (
        jnp.stack([grad_queries, grad_keys, grad_values], axis=1)
        .reshape(L, 3 * D)
        .astype(jnp.bfloat16)
    )
    bias_mixed = jnp.sum(grad_mixed_low.astype(jnp.float32), axis=0)
    input_low = row_input.astype(jnp.bfloat16)
    grad_mix = contract_rows(input_low, grad_mixed_low)
    grad_input = grad_pre_one + contract_cols(grad_mixed_low, mix_w)
    grad_vec = jnp.concatenate(
        [
            bias_mixed[None, :D],
            bias_mixed[None, 2 * D :],
            bias_out[None],
            gain_one[None],
            shift_one[None],
            bias_up.reshape(4, D),
            bias_down[None],
            gain_two[None],
            shift_two[None],
        ],
        axis=0,
    )
    return (grad_input, (grad_mix, grad_out, grad_up, grad_down, grad_vec))


def adam_update(master, grad_share, first, second, rate, factor):
    clipped = grad_share * factor
    first_new = beta_first * first + (1.0 - beta_first) * clipped
    second_new = beta_second * second + (1.0 - beta_second) * clipped * clipped
    first_hat = first_new / (1.0 - beta_first**STEP)
    second_hat = second_new / (1.0 - beta_second**STEP)
    master_new = master - rate * (
        first_hat / (jnp.sqrt(second_hat) + adam_eps) + weight_decay * master
    )
    return (master_new[None], first_new[None], second_new[None])


def body(
    tokens,
    segments,
    positives,
    token_grad,
    mix_weight,
    out_weight,
    up_weight,
    down_weight,
    vectors,
    first_mix,
    first_out,
    first_up,
    first_down,
    first_vectors,
    second_mix,
    second_out,
    second_up,
    second_down,
    second_vectors,
):
    masters = (mix_weight[0], out_weight[0], up_weight[0], down_weight[0], vectors[0])
    low_copies = tuple((master.astype(jnp.bfloat16) for master in masters))
    gathered = (
        lax.all_gather(low_copies[0], "dp", axis=0, tiled=True),
        lax.all_gather(low_copies[1], "dp", axis=0, tiled=True),
        lax.all_gather(low_copies[2], "dp", axis=0, tiled=True),
        lax.all_gather(low_copies[3], "dp", axis=0, tiled=True),
        lax.all_gather(low_copies[4], "dp", axis=1, tiled=True),
    )
    params = (gathered[0], gathered[1], gathered[2], gathered[3], gathered[4].astype(jnp.float32))
    is_passage = lax.axis_index("tower") == 1
    rows_here = tokens.shape[2]
    local_queries = rows_here * SEGS
    zero_grads = tuple((jnp.zeros(param.shape, jnp.float32) for param in params))
    totals = zero_grads
    shares = tuple((jnp.zeros(master.shape, jnp.float32) for master in masters))
    layer_rows = []
    input_rows = []
    for batch in range(MB):
        batch_tokens = tokens[0, batch].astype(jnp.float32)
        batch_segs = segments[0, batch]
        outputs, kept = lax.map(
            lambda row_pair: row_forward(params, row_pair[0], row_pair[1]),
            (batch_tokens, batch_segs),
        )
        layer_rows.append(outputs.astype(jnp.bfloat16))
        tables = jax.vmap(cls_table)(batch_segs)
        pooled = jnp.einsum("rsl,rld->rsd", tables, outputs, precision=highest).reshape(
            local_queries, D
        )
        pooled_low = pooled.astype(jnp.bfloat16)
        arrived = passed_along(pooled_low, "tower", 1)
        everyone = lax.all_gather(pooled_low, "dp", axis=0, tiled=True)
        contrast = contract_cols(arrived, everyone) * score_scale
        largest = jnp.max(contrast, axis=-1, keepdims=True)
        expo = jnp.exp(contrast - largest)
        probs = expo / jnp.sum(expo, axis=-1, keepdims=True)
        chosen = (
            jnp.arange(everyone.shape[0], dtype=jnp.int32)[None, :] == positives[batch][:, None]
        ).astype(jnp.float32)
        grad_contrast = (contrast_weight * (probs - chosen)).astype(jnp.bfloat16)
        grad_query_low = (plain_dot(grad_contrast, everyone) * score_scale).astype(jnp.bfloat16)
        passage_terms = contract_rows(grad_contrast, arrived) * score_scale
        passage_share = lax.psum_scatter(passage_terms, "dp", scatter_dimension=0, tiled=True)
        returned = passed_along(grad_query_low, "tower", -1)
        grad_pooled = jnp.where(is_passage, passage_share, returned.astype(jnp.float32)).reshape(
            rows_here, SEGS, D
        )
        upstream = token_grad[0, batch] + jnp.einsum(
            "rsl,rsd->rld", tables, grad_pooled, precision=highest
        )

        def back_step(carry, row_pack):
            row_input, seg_row, row_kept, row_upstream = row_pack
            grad_input, row_grads = row_backward(params, row_input, seg_row, row_kept, row_upstream)
            return (
                tuple((earlier + row_term for earlier, row_term in zip(carry, row_grads))),
                grad_input,
            )

        start = totals
        carried, grad_rows = lax.scan(back_step, start, (batch_tokens, batch_segs, kept, upstream))
        input_rows.append(grad_rows)
        totals = carried
    shares = (
        lax.psum_scatter(totals[0], "dp", scatter_dimension=0, tiled=True),
        lax.psum_scatter(totals[1], "dp", scatter_dimension=0, tiled=True),
        lax.psum_scatter(totals[2], "dp", scatter_dimension=0, tiled=True),
        lax.psum_scatter(totals[3], "dp", scatter_dimension=0, tiled=True),
        lax.psum_scatter(totals[4], "dp", scatter_dimension=1, tiled=True),
    )
    local_square = jnp.sum(shares[0] * shares[0])
    for index in range(1, 5):
        local_square = local_square + jnp.sum(shares[index] * shares[index])
    grad_square = lax.psum(local_square, ("tower", "dp"))
    factor = jnp.minimum(1.0, clip_norm / (jnp.sqrt(grad_square) + 1e-06))
    firsts = (first_mix[0], first_out[0], first_up[0], first_down[0], first_vectors[0])
    seconds = (second_mix[0], second_out[0], second_up[0], second_down[0], second_vectors[0])
    rates = (matrix_rate, matrix_rate, matrix_rate, matrix_rate, vector_rate)
    results = [
        adam_update(
            masters[index], shares[index], firsts[index], seconds[index], rates[index], factor
        )
        for index in range(5)
    ]
    layer_output = jnp.stack(layer_rows, axis=0)[None]
    input_grad = jnp.stack(input_rows, axis=0)[None]
    return (
        layer_output,
        input_grad,
        results[0][0],
        results[1][0],
        results[2][0],
        results[3][0],
        results[4][0],
        results[0][1],
        results[1][1],
        results[2][1],
        results[3][1],
        results[4][1],
        results[0][2],
        results[1][2],
        results[2][2],
        results[3][2],
        results[4][2],
        grad_square,
    )


def solution(mesh):
    in_specs = (
        P("tower", None, "dp", None, None),
        P("tower", None, "dp", None),
        P(None, "dp"),
        P("tower", None, "dp", None, None),
        P("tower", "dp", None),
        P("tower", "dp", None),
        P("tower", "dp", None),
        P("tower", "dp", None),
        P("tower", None, "dp"),
        P("tower", "dp", None),
        P("tower", "dp", None),
        P("tower", "dp", None),
        P("tower", "dp", None),
        P("tower", None, "dp"),
        P("tower", "dp", None),
        P("tower", "dp", None),
        P("tower", "dp", None),
        P("tower", "dp", None),
        P("tower", None, "dp"),
    )
    out_specs = (
        P("tower", None, "dp", None, None),
        P("tower", None, "dp", None, None),
        P("tower", "dp", None),
        P("tower", "dp", None),
        P("tower", "dp", None),
        P("tower", "dp", None),
        P("tower", None, "dp"),
        P("tower", "dp", None),
        P("tower", "dp", None),
        P("tower", "dp", None),
        P("tower", "dp", None),
        P("tower", None, "dp"),
        P("tower", "dp", None),
        P("tower", "dp", None),
        P("tower", "dp", None),
        P("tower", "dp", None),
        P("tower", None, "dp"),
        P(),
    )
    return jax.shard_map(body, mesh=mesh, in_specs=in_specs, out_specs=out_specs, check_vma=False)
```

profile of v0, /device:TPU:0, one launch (start us, length us, event | category | flops | bytes accessed | tf_op | source)
XLA Modules:
  0.0 980.9 jit_solution(14937504242856474466)
XLA Ops:
  14.6 23.3 %all-gather = bf16[16,48,12]{1,2,0:T(8,128)(2,1)S(1)} all-gather(bf16[1,48,12]{1,2,0:T(8,128)(2,1)S(1)} %bitcast.358), channel_id=1, replica_groups=mesh['tower'=2,'dp'=16] {'dp'}, dimensions={0}, use_global_device_ids=true | all-gather | bytes 19584 | tf_op jit(solution)/shard_map/all_gather | solution.py:249
  41.1 19.5 %all-gather.6.cloned.1.call-done = bf16[768,2304]{1,0:T(8,128)(2,1)} async-done(((bf16[48,2304]{1,0:T(8,128)(2,1)}), bf16[768,2304]{1,0:T(8,128)(2,1)}) %all-gather.6.cloned.1.call-update) | async-done | bytes 3538960 | tf_op jit(solution)/shard_map/all_gather | solution.py:245
  60.6 5.4 fusion.24
  105.3 50.8 %all-gather.10.cloned.1.call-done = bf16[768,3072]{1,0:T(8,128)(2,1)} async-done(((bf16[48,3072]{1,0:T(8,128)(2,1)}), bf16[768,3072]{1,0:T(8,128)(2,1)}) %all-gather.10.cloned.1.call-update) | async-done | bytes 4718608 | tf_op jit(solution)/shard_map/all_gather | solution.py:247
  156.1 4.8 fusion.137
  163.7 35.2 %multiply_convert_fusion.3 = (bf16[512,3072]{1,0:T(8,128)(2,1)}, f32[512,3072]{1,0:T(8,128)}, bf16[512,3072]{1,0:T(8,128)(2,1)}, f32[512,3072]{1,0:T(8,128)}, f32[512,3072]{1,0:T(8,128)}) fusion(f32[3072]{0:T(1024)S(1)} %add.395, f32[512,3072]{1,0:T(8,128)S(1)} %fusion.137, bf16[768,3072]{1,0:T(8,128)(2,1)S(1)} %copy-done.91, ...), kind=kOutput, calls=%fused_computation.42 | convolution fusion | flops 2625503232 | bytes 37771264 | tf_op jit(solution)/shard_map/while/body/eval_jaxpr/dot_general | solution.py:40
  198.9 11.9 %all-gather.12.cloned.1.call-done = bf16[3072,768]{1,0:T(8,128)(2,1)} async-done(((bf16[192,768]{1,0:T(8,128)(2,1)}), bf16[3072,768]{1,0:T(8,128)(2,1)}) %all-gather.12.cloned.1.call-update) | async-done | bytes 4718608 | tf_op jit(solution)/shard_map/all_gather | solution.py:248
  210.8 6.2 fusion.150
  227.0 19.6 %all_gather.27 = bf16[128,768]{1,0:T(8,128)(2,1)S(1)} all-gather(bf16[8,768]{1,0:T(8,128)(2,1)S(1)} %fusion.44), channel_id=1, replica_groups=mesh['tower'=2,'dp'=16] {'dp'}, dimensions={0}, use_global_device_ids=true | all-gather | bytes 208896 | tf_op jit(solution)/shard_map/all_gather | solution.py:274
  250.1 18.2 %all_gather.26 = bf16[128,768]{1,0:T(8,128)(2,1)S(1)} all-gather(bf16[8,768]{1,0:T(8,128)(2,1)} %fusion.45), channel_id=1, replica_groups=mesh['tower'=2,'dp'=16] {'dp'}, dimensions={0}, use_global_device_ids=true | all-gather | bytes 208896 | tf_op jit(solution)/shard_map/all_gather | solution.py:274
  278.8 23.1 %reduce-scatter.14.cloned.1.call-done = f32[8,768]{1,0:T(8,128)} async-done(((f32[128,768]{1,0:T(8,128)}), f32[8,768]{1,0:T(8,128)}) %reduce-scatter.14.cloned.1.call-update) | async-done | bytes 24592 | tf_op jit(solution)/shard_map/reduce_scatter | solution.py:285
  305.4 55.5 %reduce-scatter.12.cloned.1.call-done = f32[8,768]{1,0:T(8,128)} async-done(((f32[128,768]{1,0:T(8,128)}), f32[8,768]{1,0:T(8,128)}) %reduce-scatter.12.cloned.1.call-update) | async-done | bytes 24592 | tf_op jit(solution)/shard_map/reduce_scatter | solution.py:285
  367.2 9.7 convert_reduce_fusion.1
  381.2 8.6 convert_reduce_fusion
  389.9 6.6 convert_reduce_fusion.7
  401.9 7.6 fusion.28
  409.4 9.8 %multiply_reduce_fusion.1 = (f32[12,512]{1,0:T(8,128)S(1)}, f32[12,512,512]{1,2,0:T(8,128)}) fusion(f32[12,512]{1,0:T(8,128)S(1)} %copy-done.53, f32[12,512,512]{1,2,0:T(8,128)} %copy-done.1, pred[512,512]{0,1:T(8,128)(4,1)S(1)} %copy-done.18, bf16[512,12,64]{0,2,1:T(8,128)(2,1)S(1)} %bitcast.343, bf16[512,3,12,64]{0,3,2,1:T(8,128)(2,1)S(1)} %bitcast.335), kind=kOutput, calls=%fused_computation.4 | convolution fusion | flops 418375680 | bytes 27058176 | tf_op jit(solution)/shard_map/while/body/eval_jaxpr/qhd,khd->hqk/dot_general | solution.py:170
  419.3 7.0 multiply_convert_fusion.1
  436.2 7.4 fusion.31
  443.6 9.8 multiply_reduce_fusion
  453.4 7.4 multiply_convert_fusion
  482.7 4.9 add_bitcast_fusion
  487.7 8.0 copy.159
  495.8 5.4 fusion.139
  501.2 6.0 convolution_add_fusion.1
  508.6 4.8 fusion.122
  513.4 5.3 convolution_add_fusion
  530.6 64.6 %reduce-scatter.16.cloned.1.call-done = f32[48,768]{1,0:T(8,128)} async-done(((f32[768,768]{1,0:T(8,128)}), f32[48,768]{1,0:T(8,128)}) %reduce-scatter.16.cloned.1.call-update) | async-done | bytes 147472 | tf_op jit(solution)/shard_map/reduce_scatter | solution.py:308
  596.7 91.6 %reduce-scatter.22.cloned.1.call-done = f32[48,2304]{1,0:T(8,128)} async-done(((f32[768,2304]{1,0:T(8,128)}), f32[48,2304]{1,0:T(8,128)}) %reduce-scatter.22.cloned.1.call-update) | async-done | bytes 442384 | tf_op jit(solution)/shard_map/reduce_scatter | solution.py:307
  692.0 111.7 %reduce-scatter.18.cloned.1.call-done = f32[48,3072]{1,0:T(8,128)} async-done(((f32[768,3072]{1,0:T(8,128)}), f32[48,3072]{1,0:T(8,128)}) %reduce-scatter.18.cloned.1.call-update) | async-done | bytes 589840 | tf_op jit(solution)/shard_map/reduce_scatter | solution.py:309
  806.2 112.7 %reduce-scatter.20.cloned.1.call-done = f32[192,768]{1,0:T(8,128)} async-done(((f32[3072,768]{1,0:T(8,128)}), f32[192,768]{1,0:T(8,128)}) %reduce-scatter.20.cloned.1.call-update) | async-done | bytes 589840 | tf_op jit(solution)/shard_map/reduce_scatter | solution.py:310
  923.4 40.2 %psum.7 = f32[]{:T(128)} all-reduce(f32[]{:T(128)S(6)} %add.433), channel_id=1, replica_groups=mesh['tower'=2,'dp'=16] {'tower','dp'}, use_global_device_ids=true, to_apply=%region_56.57 | all-reduce | flops 1 | bytes 8 | tf_op jit(solution)/shard_map/psum | solution.py:316
  (372 shorter events, 158.6 us)
Async XLA Ops:
  7.2 53.4 %all-gather.6.cloned.1.call-start = ((), (), s32[]{:S(2)}) async-start(), calls=%async_computation.7 | async-start | bytes 3760128 | tf_op jit(solution)/shard_map/all_gather | solution.py:245
  9.1 91.7 %all-gather.8.cloned.1.call-start = ((), (), s32[]{:S(2)}) async-start(), calls=%async_computation.8 | async-start | bytes 1253376 | tf_op jit(solution)/shard_map/all_gather | solution.py:246
  10.8 145.3 %all-gather.10.cloned.1.call-start = ((), (), s32[]{:S(2)}) async-start(), calls=%async_computation.9 | async-start | bytes 5013504 | tf_op jit(solution)/shard_map/all_gather | solution.py:247
  12.7 198.1 %all-gather.12.cloned.1.call-start = ((), (), s32[]{:S(2)}) async-start(), calls=%async_computation.10 | async-start | bytes 5013504 | tf_op jit(solution)/shard_map/all_gather | solution.py:248
  14.5 287.4 %reduce-scatter.14.cloned.1.call-start = ((), (), s32[]{:S(2)}) async-start(), calls=%async_computation.12 | async-start | bytes 417792 | tf_op jit(solution)/shard_map/reduce_scatter | solution.py:285
  41.1 119.9 %copy-start.72 = (f32[3072]{0:T(1024)}, f32[3072]{0:T(1024)S(1)}, u32[]{:S(2)}) copy-start(f32[3072]{0:T(1024)S(1)} %add.395) | copy-start | bytes 36868
  103.6 107.1 %copy-start.39 = (f32[512,768]{1,0:T(8,128)}, f32[512,768]{1,0:T(8,128)S(1)}, u32[]{:S(2)}) copy-start(f32[512,768]{1,0:T(8,128)S(1)} %get-tuple-element.453) | copy-start | bytes 4718596
  103.7 107.1 %copy-start.74 = (f32[512]{0:T(512)}, f32[512]{0:T(512)S(1)}, u32[]{:S(2)}) copy-start(f32[512]{0:T(512)S(1)} %broadcast_multiply_fusion.11) | copy-start | bytes 6148
  104.0 106.8 %copy-start.88 = (f32[512]{0:T(512)}, f32[512]{0:T(512)S(1)}, u32[]{:S(2)}) copy-start(f32[512]{0:T(512)S(1)} %add_rsqrt_fusion.3) | copy-start | bytes 6148
  105.0 112.4 %copy-start.56 = (f32[512]{0:T(512)}, f32[512]{0:T(512)S(1)}, u32[]{:S(2)}) copy-start(f32[512]{0:T(512)S(1)} %broadcast_multiply_fusion.9) | copy-start | bytes 6148
  105.3 112.1 %copy-start.64 = (f32[512]{0:T(512)}, f32[512]{0:T(512)S(1)}, u32[]{:S(2)}) copy-start(f32[512]{0:T(512)S(1)} %add_rsqrt_fusion.1) | copy-start | bytes 6148
  222.1 26.4 %collective-permute-start.2 = (bf16[8,768]{1,0:T(8,128)(2,1)S(1)}, bf16[8,768]{1,0:T(8,128)(2,1)S(1)}, u32[]{:S(2)}, u32[]{:S(2)}) collective-permute-start(bf16[8,768]{1,0:T(8,128)(2,1)S(1)} %fusion.44), channel_id=1, source_target_pairs={{0,16},{1,17},{2,18},{3,19},{4,20},{5,21},{6,22},{7,23},{8,24},{9,... | collective-permute-start | bytes 36872 | tf_op jit(solution)/shard_map/ppermute | solution.py:36
  246.6 21.8 %collective-permute-start = (bf16[8,768]{1,0:T(8,128)(2,1)}, bf16[8,768]{1,0:T(8,128)(2,1)}, u32[]{:S(2)}, u32[]{:S(2)}) collective-permute-start(bf16[8,768]{1,0:T(8,128)(2,1)} %fusion.45), channel_id=1, source_target_pairs={{0,16},{1,17},{2,18},{3,19},{4,20},{5,21},{6,22},{7,23},{8,24},{9,... | collective-permute-start | bytes 36872 | tf_op jit(solution)/shard_map/ppermute | solution.py:36
  250.1 110.8 %reduce-scatter.12.cloned.1.call-start = ((), (), s32[]{:S(2)}) async-start(), calls=%async_computation.11 | async-start | bytes 417792 | tf_op jit(solution)/shard_map/reduce_scatter | solution.py:285
  271.9 257.2 %reduce-scatter.24.cloned.1.call-start = ((), (), s32[]{:S(2)}) async-start(), calls=%async_computation.17 | async-start | bytes 417792
  273.0 87.9 %copy-start.59 = (f32[512]{0:T(512)S(1)}, f32[512]{0:T(512)}, u32[]{:S(2)}) copy-start(f32[512]{0:T(512)} %copy-done.58) | copy-start | bytes 6148
  273.0 87.9 %copy-start.61 = (f32[512]{0:T(512)S(1)}, f32[512]{0:T(512)}, u32[]{:S(2)}) copy-start(f32[512]{0:T(512)} %copy-done.60) | copy-start | bytes 6148
  273.0 87.8 %copy-start.67 = (f32[512]{0:T(512)S(1)}, f32[512]{0:T(512)}, u32[]{:S(2)}) copy-start(f32[512]{0:T(512)} %copy-done.66) | copy-start | bytes 6148
  273.1 5.7 collective-permute-start.3
  275.4 30.0 %collective-permute-start.1 = (bf16[8,768]{1,0:T(8,128)(2,1)S(1)}, bf16[8,768]{1,0:T(8,128)(2,1)S(1)}, u32[]{:S(2)}, u32[]{:S(2)}) collective-permute-start(bf16[8,768]{1,0:T(8,128)(2,1)S(1)} %fusion.42), channel_id=1, source_target_pairs={{16,0},{17,1},{18,2},{19,3},{20,4},{21,5},{22,6},{23,7},{24,8},{25... | collective-permute-start | bytes 36872 | tf_op jit(solution)/shard_map/ppermute | solution.py:36
  474.2 121.0 %reduce-scatter.16.cloned.1.call-start = ((), (), s32[]{:S(2)}) async-start(), calls=%async_computation.13 | async-start | bytes 2506752 | tf_op jit(solution)/shard_map/reduce_scatter | solution.py:308
  478.6 209.7 %reduce-scatter.22.cloned.1.call-start = ((), (), s32[]{:S(2)}) async-start(), calls=%async_computation.16 | async-start | bytes 7520256 | tf_op jit(solution)/shard_map/reduce_scatter | solution.py:307
  495.7 308.0 %reduce-scatter.18.cloned.1.call-start = ((), (), s32[]{:S(2)}) async-start(), calls=%async_computation.14 | async-start | bytes 10027008 | tf_op jit(solution)/shard_map/reduce_scatter | solution.py:309
  507.2 411.7 %reduce-scatter.20.cloned.1.call-start = ((), (), s32[]{:S(2)}) async-start(), calls=%async_computation.15 | async-start | bytes 10027008 | tf_op jit(solution)/shard_map/reduce_scatter | solution.py:310
  529.1 393.0 %copy-start.28 = (bf16[1,1,512,768]{3,2,1,0:T(8,128)(2,1)S(1)}, bf16[1,1,512,768]{3,2,1,0:T(8,128)(2,1)}, u32[]{:S(2)}) copy-start(bf16[1,1,512,768]{3,2,1,0:T(8,128)(2,1)} %get-tuple-element.413) | copy-start | bytes 2359300
  529.1 393.0 %copy-start.29 = (bf16[1,1,512,768]{3,2,1,0:T(8,128)(2,1)S(1)}, bf16[1,1,512,768]{3,2,1,0:T(8,128)(2,1)}, u32[]{:S(2)}) copy-start(bf16[1,1,512,768]{3,2,1,0:T(8,128)(2,1)} %get-tuple-element.435) | copy-start | bytes 2359300
  689.7 274.6 %copy-start.71 = (f32[1,12,48]{2,0,1:T(1,128)S(1)}, f32[1,12,48]{2,0,1:T(1,128)}, u32[]{:S(2)}) copy-start(f32[1,12,48]{2,0,1:T(1,128)} %param.27) | copy-start | bytes 6916
  689.7 274.6 %copy-start.76 = (f32[1,12,48]{2,0,1:T(1,128)S(1)}, f32[1,12,48]{2,0,1:T(1,128)}, u32[]{:S(2)}) copy-start(f32[1,12,48]{2,0,1:T(1,128)} %param.37) | copy-start | bytes 6916
  689.7 274.6 %copy-start.77 = (f32[1,12,48]{2,0,1:T(1,128)S(1)}, f32[1,12,48]{2,0,1:T(1,128)}, u32[]{:S(2)}) copy-start(f32[1,12,48]{2,0,1:T(1,128)} %param.32) | copy-start | bytes 6916
  689.8 276.4 %copy-start.50 = (f32[1,48,768]{2,1,0:T(8,128)S(1)}, f32[1,48,768]{2,1,0:T(8,128)}, u32[]{:S(2)}) copy-start(f32[1,48,768]{2,1,0:T(8,128)} %param.24) | copy-start | bytes 442372
  689.8 276.4 %copy-start.51 = (f32[48,768]{1,0:T(8,128)S(1)}, f32[48,768]{1,0:T(8,128)}, u32[]{:S(2)}) copy-start(f32[48,768]{1,0:T(8,128)} %reduce-scatter.16.cloned.1.call-done) | copy-start | bytes 442372
  689.8 278.2 %copy-start.34 = (f32[48,2304]{1,0:T(8,128)S(1)}, f32[48,2304]{1,0:T(8,128)}, u32[]{:S(2)}) copy-start(f32[48,2304]{1,0:T(8,128)} %reduce-scatter.22.cloned.1.call-done) | copy-start | bytes 1327108
  (91 other events, 1155.2 us)
Sparse Core Ops, SparseCore 0:
  10.9 49.6 all-gather.5
  63.5 37.3 all-gather.7
  103.7 52.3 all-gather.9
  158.8 51.9 all-gather.11
  250.2 51.6 reduce-scatter.13
  306.3 54.5 reduce-scatter.11
  474.3 54.5 reduce-scatter.23
  533.2 61.9 reduce-scatter.15
  599.2 89.0 reduce-scatter.21
  692.8 110.8 reduce-scatter.17
  807.8 111.0 reduce-scatter.19
where the time goes:
time: 990 us; the launch traced here: 981 us
  waiting for transfers between devices  547 us (55%)
  matrix products  211 us (21%)
  blocking collectives  101 us (10%)
  other arithmetic  59.9 us (6%)
  local copies, waits for them, and re-layouts  33.6 us (3%)
  between operations  19.6 us (2%)
    reduce_scatter x1, waiting for transfers between devices, body(): lax.psum_scatter(totals[3], 'dp', scatter_dimension=0, tiled=True)  113 us
    reduce_scatter x1, waiting for transfers between devices, body(): lax.psum_scatter(totals[2], 'dp', scatter_dimension=0, tiled=True)  112 us
    reduce_scatter x1, waiting for transfers between devices, body(): lax.psum_scatter(totals[0], 'dp', scatter_dimension=0, tiled=True)  91.6 us
    reduce_scatter x2, waiting for transfers between devices, body(): lax.psum_scatter(passage_terms, 'dp', scatter_dimension=0, tiled=True)  78.6 us
    reduce_scatter x1, waiting for transfers between devices, body(): lax.psum_scatter(totals[1], 'dp', scatter_dimension=0, tiled=True)  64.6 us
    dot_general x10, matrix products, plain_dot(): return jnp.dot(first_op, second_op, preferred_element_type=jnp.float32)  63.3 us
    all_gather x1, waiting for transfers between devices, body(): lax.all_gather(low_copies[2], 'dp', axis=0, tiled=True)  50.8 us
    dot_general x10, matrix products, contract_cols(): lax.dot_general(first_op, second_op, (((1,), (1,)), ((), ())), preferred_...  40.6 us
  transfers between devices with their start and end apart: 15, of which 11 were waited for; matrix products, arithmetic and copies ran while one was open for 16% of the time, Pallas kernels for 0%

commit v1 on v0

v1 whole, which is shorter than its diff:
```python
from functools import partial

import jax
import jax.numpy as jnp
from jax import lax
from jax.sharding import PartitionSpec as P

D = 768
FF = 3072
H = 12
HD = 64
L = 512
SEGS = 8
MB = 2
STEP = 5
HG = 3
PIECES = 16
PIECE_ROWS = D // PIECES

norm_eps = 1e-05
attention_scale = 0.125
score_scale = 0.0625
contrast_weight = 16.0
clip_norm = 1.0
beta_first = 0.9
beta_second = 0.999
adam_eps = 1e-08
weight_decay = 0.01
matrix_rate = 0.05
vector_rate = 0.5
masked_score = -1e30

low_type = jnp.bfloat16
highest = lax.Precision.HIGHEST


def swapped(value, mask):
    pairs = [(i, i ^ mask) for i in range(lax.axis_size("dp"))]
    return lax.ppermute(value, "dp", pairs)


def tower_swapped(value):
    return lax.ppermute(value, "tower", [(0, 1), (1, 0)])


def relative_of(place):
    return ((place & 3) << 2) | (((place >> 2) & 1) << 1) | (place >> 3)


def place_of(relative):
    return ((relative & 1) << 3) | (((relative >> 1) & 1) << 2) | (relative >> 2)


def gather_pieces(own):
    four = jnp.stack([own, swapped(own, 4), swapped(own, 8), swapped(own, 12)])
    eight = jnp.concatenate([four, swapped(four, 2)])
    return jnp.concatenate([eight, swapped(eight, 1)])


def scatter_pieces(pieces):
    eight = added(pieces[:8], swapped(pieces[8:], 1)).astype(low_type)
    four = added(eight[:4], swapped(eight[4:], 2)).astype(low_type)
    total = added(four[0], swapped(four[1], 4))
    total = total + swapped(four[2], 8).astype(jnp.float32)
    return total + swapped(four[3], 12).astype(jnp.float32)


def added(first, second):
    return first.astype(jnp.float32) + second.astype(jnp.float32)


def plain_dot(first_op, second_op):
    return jnp.dot(first_op, second_op, preferred_element_type=jnp.float32)


def contract_rows(first_op, second_op):
    return lax.dot_general(
        first_op, second_op, (((0,), (0,)), ((), ())), preferred_element_type=jnp.float32
    )


def contract_cols(first_op, second_op):
    return lax.dot_general(
        first_op, second_op, (((1,), (1,)), ((), ())), preferred_element_type=jnp.float32
    )


def layer_stats(values):
    centred = values - jnp.mean(values, axis=-1, keepdims=True)
    inverse = lax.rsqrt(jnp.mean(centred * centred, axis=-1, keepdims=True) + norm_eps)
    return (centred * inverse, inverse)


def norm_back(upstream, normed, inverse, gain_row):
    gained = upstream * gain_row
    return inverse * (
        gained
        - jnp.mean(gained, axis=-1, keepdims=True)
        - normed * jnp.mean(gained * normed, axis=-1, keepdims=True)
    )


def cls_table(seg_row):
    starts = jnp.sum(
        (seg_row[None, :] < jnp.arange(SEGS, dtype=jnp.int32)[:, None]).astype(jnp.int32), axis=1
    )
    return (jnp.arange(L, dtype=jnp.int32)[None, :] == starts[:, None]).astype(jnp.float32)


def attention_scores(queries, key_rows, seg_rows):
    scores = (
        jnp.einsum("bqhd,bkhd->bhqk", queries, key_rows, preferred_element_type=jnp.float32)
        * attention_scale
    )
    same_doc = seg_rows[:, :, None] == seg_rows[:, None, :]
    return jnp.where(same_doc[:, None], scores, masked_score)


def by_heads(matrix):
    shaped = matrix.reshape(matrix.shape[0], 3, HG, D // HG)
    return jnp.transpose(shaped, (2, 0, 1, 3)).reshape(HG, matrix.shape[0], D)


def from_heads(blocks):
    rows = blocks.shape[1]
    shaped = blocks.reshape(HG, rows, 3, D // HG)
    return jnp.transpose(shaped, (1, 2, 0, 3)).reshape(rows, 3 * D)


def by_columns(matrix):
    return jnp.transpose(matrix.reshape(matrix.shape[0], 4, D), (1, 0, 2))


def from_columns(blocks):
    return jnp.transpose(blocks, (1, 0, 2)).reshape(blocks.shape[1], 4 * D)


def adam_update(master, grad_share, first, second, rate, factor):
    clipped = grad_share * factor
    first_new = beta_first * first + (1.0 - beta_first) * clipped
    second_new = beta_second * second + (1.0 - beta_second) * clipped * clipped
    first_hat = first_new / (1.0 - beta_first**STEP)
    second_hat = second_new / (1.0 - beta_second**STEP)
    master_new = master - rate * (
        first_hat / (jnp.sqrt(second_hat) + adam_eps) + weight_decay * master
    )
    return (master_new[None], first_new[None], second_new[None])


def body(
    tokens,
    segments,
    positives,
    token_grad,
    mix_weight,
    out_weight,
    up_weight,
    down_weight,
    vectors,
    first_mix,
    first_out,
    first_up,
    first_down,
    first_vectors,
    second_mix,
    second_out,
    second_up,
    second_down,
    second_vectors,
):
    owners = lax.axis_size("dp")
    fast = owners == PIECES
    me = lax.axis_index("dp")
    is_passage = lax.axis_index("tower") == 1
    masters = (mix_weight[0], out_weight[0], up_weight[0], down_weight[0], vectors[0])
    low_mix, low_out, low_up, low_down, low_vec = (m.astype(low_type) for m in masters)
    share = low_vec.shape[1]
    queries_all = owners * SEGS

    if fast:
        extra = jnp.zeros((16, D), low_type)
        extra = extra.at[12:14, :SEGS].set(positives.astype(low_type))
        extra = lax.dynamic_update_slice(extra, low_vec, (0, me * share))
        pack_mix = jnp.concatenate([by_heads(low_mix).reshape(-1, D), extra])
        got_mix = gather_pieces(pack_mix)
        got_up = gather_pieces(jnp.concatenate([low_out, by_columns(low_up).reshape(-1, D)]))
        got_down = gather_pieces(low_down)
        places = place_of(jnp.arange(PIECES, dtype=jnp.int32) ^ me)
        vec_f = jnp.sum(got_mix[:, 144:156].astype(jnp.float32), axis=0)
        cls_positives = got_mix[:, 156:158, :SEGS].astype(jnp.int32)
        cls_positives = jnp.transpose(cls_positives, (1, 0, 2)).reshape(MB, queries_all)
        got_mix, got_up, got_down = (jnp.take(g, places, axis=0) for g in (got_mix, got_up, got_down))
        mix_w = from_heads(
            jnp.transpose(got_mix[:, :144].reshape(PIECES, HG, PIECE_ROWS, D), (1, 0, 2, 3)).reshape(
                HG, D, D
            )
        )
        out_w = got_up[:, :48].reshape(D, D)
        up_w = from_columns(
            jnp.transpose(got_up[:, 48:].reshape(PIECES, 4, PIECE_ROWS, D), (1, 0, 2, 3)).reshape(
                4, D, D
            )
        )
        down_w = got_down.reshape(FF, D)
        relative = relative_of(jnp.arange(PIECES, dtype=jnp.int32))
        cls_ids = ((relative ^ me)[:, None] * SEGS + jnp.arange(SEGS)[None, :]).reshape(-1)
    else:
        mix_w = lax.all_gather(low_mix, "dp", axis=0, tiled=True)
        out_w = lax.all_gather(low_out, "dp", axis=0, tiled=True)
        up_w = lax.all_gather(low_up, "dp", axis=0, tiled=True)
        down_w = lax.all_gather(low_down, "dp", axis=0, tiled=True)
        vec_f = lax.all_gather(low_vec, "dp", axis=1, tiled=True).astype(jnp.float32)
        cls_positives = jnp.roll(
            lax.all_gather(positives, "dp", axis=1, tiled=True), -me * SEGS, axis=1
        )
        cls_ids = jnp.roll(jnp.arange(queries_all, dtype=jnp.int32), -me * SEGS)

    x_low = tokens[0].reshape(MB * L, D)
    x_f = x_low.astype(jnp.float32)
    seg_rows = segments[0].reshape(MB, L)
    mixed_bias = jnp.concatenate([vec_f[0], jnp.zeros_like(vec_f[0]), vec_f[1]])
    mixed_low = (plain_dot(x_low, mix_w) + mixed_bias).astype(low_type)
    shaped = mixed_low.reshape(MB, L, 3, H, HD)
    queries, key_rows, value_rows = shaped[:, :, 0], shaped[:, :, 1], shaped[:, :, 2]
    scores = attention_scores(queries, key_rows, seg_rows)
    largest = jnp.max(scores, axis=-1, keepdims=True)
    expo = jnp.exp(scores - largest)
    summed = jnp.sum(expo, axis=-1, keepdims=True)
    probs = expo / summed
    log_total = (largest + jnp.log(summed))[..., 0]
    context = jnp.einsum(
        "bhqk,bkhd->bqhd", probs.astype(low_type), value_rows, preferred_element_type=jnp.float32
    )
    context_low = context.reshape(MB * L, D).astype(low_type)
    branch = plain_dot(context_low, out_w) + vec_f[2]
    normed_one, inverse_one = layer_stats(x_f + branch)
    hidden = normed_one * vec_f[3] + vec_f[4]
    hidden_low = hidden.astype(low_type)
    pre_act = plain_dot(hidden_low, up_w) + vec_f[5:9].reshape(FF)
    active_low = jax.nn.gelu(pre_act, approximate=False).astype(low_type)
    ffn_out = plain_dot(active_low, down_w) + vec_f[9]
    normed_two, inverse_two = layer_stats(hidden + ffn_out)
    output = normed_two * vec_f[10] + vec_f[11]

    tables = jax.vmap(cls_table)(seg_rows)
    pooled = jnp.einsum("rsl,rld->rsd", tables, output.reshape(MB, L, D), precision=highest)
    pooled_low = pooled.astype(low_type).reshape(MB * SEGS, D)
    both = jnp.concatenate([pooled_low, tower_swapped(pooled_low)])
    if fast:
        everyone = gather_pieces(both)
    else:
        everyone = lax.all_gather(both, "dp", axis=0, tiled=False)
        everyone = jnp.roll(everyone, -me, axis=0)
    everyone = jnp.transpose(everyone.reshape(owners, 2, MB, SEGS, D), (1, 2, 0, 3, 4))
    everyone = everyone.reshape(2, MB, queries_all, D)
    cls_query = jnp.where(is_passage, everyone[1], everyone[0])
    cls_passage = jnp.where(is_passage, everyone[0], everyone[1])
    contrast = (
        jnp.einsum("mqd,mpd->mqp", cls_query, cls_passage, preferred_element_type=jnp.float32)
        * score_scale
    )
    top = jnp.max(contrast, axis=-1, keepdims=True)
    cexpo = jnp.exp(contrast - top)
    cprobs = cexpo / jnp.sum(cexpo, axis=-1, keepdims=True)
    chosen = (cls_ids[None, None, :] == cls_positives[:, :, None]).astype(jnp.float32)
    grad_contrast = (contrast_weight * (cprobs - chosen)).astype(low_type)
    mine = jnp.where(
        is_passage, jnp.transpose(grad_contrast[:, :, :SEGS], (0, 2, 1)), grad_contrast[:, :SEGS]
    )
    theirs = jnp.where(is_passage, cls_query, cls_passage)
    grad_cls = (
        jnp.einsum("msq,mqd->msd", mine, theirs, preferred_element_type=jnp.float32) * score_scale
    )
    grad_cls = jnp.where(is_passage, grad_cls, grad_cls.astype(low_type).astype(jnp.float32))
    upstream = token_grad[0].reshape(MB, L, D) + jnp.einsum(
        "rsl,rsd->rld", tables, grad_cls, precision=highest
    )
    upstream = upstream.reshape(MB * L, D)

    def spread(blocks):
        order = relative_of(jnp.arange(PIECES, dtype=jnp.int32)) ^ me
        k = blocks.shape[0]
        shaped = jnp.transpose(blocks.reshape(k, PIECES, PIECE_ROWS, D), (1, 0, 2, 3))
        return jnp.take(shaped.reshape(PIECES, k * PIECE_ROWS, D), order, axis=0)

    gain_two = jnp.sum(upstream * normed_two, axis=0)
    shift_two = jnp.sum(upstream, axis=0)
    grad_pre_two = norm_back(upstream, normed_two, inverse_two, vec_f[10])
    grad_ffn_low = grad_pre_two.astype(low_type)
    bias_down = jnp.sum(grad_ffn_low.astype(jnp.float32), axis=0)
    grad_down = contract_rows(active_low, grad_ffn_low)
    if fast:
        order = relative_of(jnp.arange(PIECES, dtype=jnp.int32)) ^ me
        share_down = scatter_pieces(
            jnp.take(grad_down.astype(low_type).reshape(PIECES, -1, D), order, axis=0)
        )
    else:
        share_down = lax.psum_scatter(grad_down, "dp", scatter_dimension=0, tiled=True)
    grad_active = contract_cols(grad_ffn_low, down_w)
    gelu_pull = jax.vjp(partial(jax.nn.gelu, approximate=False), pre_act)[1]
    grad_pre_low = gelu_pull(grad_active)[0].astype(low_type)
    bias_up = jnp.sum(grad_pre_low.astype(jnp.float32), axis=0)
    grad_up = contract_rows(hidden_low, grad_pre_low)
    if fast:
        share_up = scatter_pieces(spread(by_columns(grad_up.astype(low_type))))
        share_up = from_columns(share_up.reshape(4, PIECE_ROWS, D))
    else:
        share_up = lax.psum_scatter(grad_up, "dp", scatter_dimension=0, tiled=True)
    grad_hidden = grad_pre_two + contract_cols(grad_pre_low, up_w)
    gain_one = jnp.sum(grad_hidden * normed_one, axis=0)
    shift_one = jnp.sum(grad_hidden, axis=0)
    grad_pre_one = norm_back(grad_hidden, normed_one, inverse_one, vec_f[3])
    grad_branch_low = grad_pre_one.astype(low_type)
    bias_out = jnp.sum(grad_branch_low.astype(jnp.float32), axis=0)
    grad_out = contract_rows(context_low, grad_branch_low)
    grad_context = contract_cols(grad_branch_low, out_w).astype(low_type).reshape(MB, L, H, HD)
    scores = attention_scores(queries, key_rows, seg_rows)
    probs = jnp.exp(scores - log_total[..., None])
    grad_values = jnp.einsum(
        "bhqk,bqhd->bkhd",
        probs.astype(low_type),
        grad_context,
        preferred_element_type=jnp.float32,
    )
    grad_probs = jnp.einsum(
        "bqhd,bkhd->bhqk", grad_context, value_rows, preferred_element_type=jnp.float32
    )
    grad_scores = probs * (grad_probs - jnp.sum(probs * grad_probs, axis=-1, keepdims=True))
    grad_scores_low = grad_scores.astype(low_type)
    grad_queries = (
        jnp.einsum("bhqk,bkhd->bqhd", grad_scores_low, key_rows, preferred_element_type=jnp.float32)
        * attention_scale
    )
    grad_keys = (
        jnp.einsum("bhqk,bqhd->bkhd", grad_scores_low, queries, preferred_element_type=jnp.float32)
        * attention_scale
    )
    grad_mixed_low = (
        jnp.stack([grad_queries, grad_keys, grad_values], axis=2)
        .reshape(MB * L, 3 * D)
        .astype(low_type)
    )
    bias_mixed = jnp.sum(grad_mixed_low.astype(jnp.float32), axis=0)
    grad_mix = contract_rows(x_low, grad_mixed_low)
    input_grad = grad_pre_one + contract_cols(grad_mixed_low, mix_w)
    grad_vec = jnp.concatenate(
        [
            bias_mixed[None, :D],
            bias_mixed[None, 2 * D :],
            bias_out[None],
            gain_one[None],
            shift_one[None],
            bias_up.reshape(4, D),
            bias_down[None],
            gain_two[None],
            shift_two[None],
        ],
        axis=0,
    )
    if fast:
        vec_rows = jnp.broadcast_to(
            jnp.pad(grad_vec, ((0, 4), (0, 0))).astype(low_type)[None], (PIECES, 16, D)
        )
        pieces = jnp.concatenate(
            [
                spread(grad_out.astype(low_type)[None]),
                spread(by_heads(grad_mix.astype(low_type))),
                vec_rows,
            ],
            axis=1,
        )
        share_rest = scatter_pieces(pieces)
        share_out = share_rest[:48]
        share_mix = from_heads(share_rest[48:192].reshape(HG, PIECE_ROWS, D))
        share_vec = lax.dynamic_slice(share_rest[192:204], (0, me * share), (12, share))
    else:
        share_mix = lax.psum_scatter(grad_mix, "dp", scatter_dimension=0, tiled=True)
        share_out = lax.psum_scatter(grad_out, "dp", scatter_dimension=0, tiled=True)
        share_vec = lax.psum_scatter(grad_vec, "dp", scatter_dimension=1, tiled=True)

    shares = (share_mix, share_out, share_up, share_down, share_vec)
    local_square = sum(jnp.sum(s * s) for s in shares)
    if fast:
        grad_square = jnp.broadcast_to(local_square, (8, 128))
        for mask in (1, 2, 4, 8):
            grad_square = grad_square + swapped(grad_square, mask)
        grad_square = grad_square + tower_swapped(grad_square)
        grad_square = grad_square[0, 0]
    else:
        grad_square = lax.psum(local_square, ("tower", "dp"))
    factor = jnp.minimum(1.0, clip_norm / (jnp.sqrt(grad_square) + 1e-06))
    firsts = (first_mix[0], first_out[0], first_up[0], first_down[0], first_vectors[0])
    seconds = (second_mix[0], second_out[0], second_up[0], second_down[0], second_vectors[0])
    rates = (matrix_rate, matrix_rate, matrix_rate, matrix_rate, vector_rate)
    results = [
        adam_update(masters[i], shares[i], firsts[i], seconds[i], rates[i], factor)
        for i in range(5)
    ]
    layer_output = output.astype(low_type).reshape(1, MB, 1, L, D)
    return (
        layer_output,
        input_grad.reshape(1, MB, 1, L, D),
        *(r[0] for r in results),
        *(r[1] for r in results),
        *(r[2] for r in results),
        grad_square,
    )


def solution(mesh):
    rows = P("tower", None, "dp", None, None)
    shards = (P("tower", "dp", None),) * 4 + (P("tower", None, "dp"),)
    in_specs = (rows, P("tower", None, "dp", None), P(None, "dp"), rows) + shards * 3
    out_specs = (rows, rows) + shards * 3 + (P(),)
    return jax.shard_map(body, mesh=mesh, in_specs=in_specs, out_specs=out_specs, check_vma=False)
```

time: 990 us -> 740 us (0.75)
  waiting for transfers between devices: 547 us -> 216 us
  local copies, waits for them, and re-layouts: 33.6 us -> 163 us
  blocking collectives: 101 us -> 0 us
  starting transfers between devices: 8.59 us -> 49.7 us
  other arithmetic: 59.9 us -> 98.7 us
  matrix products: 211 us -> 196 us
  between operations: 19.6 us -> 6.41 us
    reduce_scatter x6 -> x0, waiting for transfers between devices: 459 us -> none  [the longest x1 113 us: body(): lax.psum_scatter(totals[3], 'dp', scatter_dimension=0, tiled=True)]
    ppermute x4 -> x41, waiting for transfers between devices: 2.08 us -> 216 us  [the longest x39 214 us: swapped(): return lax.ppermute(value, 'dp', pairs)]
    all_gather x4 -> x0, waiting for transfers between devices: 85.8 us -> none  [the longest x1 50.8 us: body(): lax.all_gather(low_copies[2], 'dp', axis=0, tiled=True)]
    all_gather x3 -> x0, blocking collectives: 61.1 us -> none  [the longest x2 37.8 us: body(): everyone = lax.all_gather(pooled_low, 'dp', axis=0, tiled=True)]
    ppermute x4 -> x41, starting transfers between devices: 7.96 us -> 49.7 us  [the longest x39 46.6 us: swapped(): return lax.ppermute(value, 'dp', pairs)]
    psum x1 -> x0, blocking collectives: 40.2 us -> none  [body(): grad_square = lax.psum(local_square, ('tower', 'dp'))]
    gather x0 -> x7, local copies, waits for them, and re-layouts: none -> 31.3 us  [the longest x3 16.7 us: body(): jnp.take(g, places, axis=0)]
    another operation x1 -> x3, local copies, waits for them, and re-layouts: 0.01 us -> 23.3 us  [the longest x1 9.35 us: body(): jnp.stack([grad_queries, grad_keys, grad_values], axis=2)]
  transfers between devices with their start and end apart: 15 -> 41, of which waited for: 11 -> 21; matrix products, arithmetic and copies ran while one was open for 16% -> 27% of each run, Pallas kernels for 0% -> 0%
where the time goes in v1:
time: 740 us; the launch traced here: 729 us
  waiting for transfers between devices  216 us (29%)
  matrix products  196 us (26%)
  local copies, waits for them, and re-layouts  163 us (22%)
  other arithmetic  98.7 us (13%)
  starting transfers between devices  49.7 us (7%)
    ppermute x39, waiting for transfers between devices, swapped(): return lax.ppermute(value, 'dp', pairs)  214 us
    dot_general x4, matrix products, plain_dot(): return jnp.dot(first_op, second_op, preferred_element_type=jnp.float32)  54.4 us
    ppermute x39, starting transfers between devices, swapped(): return lax.ppermute(value, 'dp', pairs)  46.6 us
    dot_general x4, matrix products, contract_cols(): lax.dot_general(first_op, second_op, (((1,), (1,)), ((), ())), preferred_...  40.7 us
    unnamed x196, local copies, waits for them, and re-layouts  26.5 us
    convert_element_type x1, other arithmetic, body(): grad_scores_low = grad_scores.astype(low_type)  21.5 us
    dot_general x4, matrix products, contract_rows(): lax.dot_general(first_op, second_op, (((0,), (0,)), ((), ())), preferred_...  21 us
    dot_general x1, matrix products, body(): jnp.einsum('bqhd,bkhd->bhqk', grad_context, value_rows, preferred_element...  18.2 us
  transfers between devices with their start and end apart: 41, of which 21 were waited for; matrix products, arithmetic and copies ran while one was open for 27% of the time, Pallas kernels for 0%

profile of v1, /device:TPU:0, one launch (start us, length us, event | category | flops | bytes accessed | tf_op | source)
XLA Modules:
  0.0 729.1 jit_solution(11721467732789397845)
XLA Ops:
  24.0 25.7 %collective-permute-done.1 = bf16[160,768]{1,0:T(8,128)(2,1)S(1)} collective-permute-done((bf16[160,768]{1,0:T(8,128)(2,1)}, bf16[160,768]{1,0:T(8,128)(2,1)S(1)}, u32[]{:S(2)}, u32[]{:S(2)}) %collective-permute-start.1) | collective-permute-done | bytes 245792 | tf_op jit(solution)/shard_map/ppermute | solution.py:39
  68.2 10.7 %collective-permute-done.3 = bf16[4,160,768]{2,1,0:T(8,128)(2,1)S(1)} collective-permute-done((bf16[4,160,768]{2,1,0:T(8,128)(2,1)}, bf16[4,160,768]{2,1,0:T(8,128)(2,1)S(1)}, u32[]{:S(2)}, u32[]{:S(2)}) %collective-permute-start.3) | collective-permute-done | bytes 983072 | tf_op jit(solution)/shard_map/ppermute | solution.py:39
  88.6 15.7 %collective-permute-done.13 = bf16[4,192,768]{2,1,0:T(8,128)(2,1)S(1)} collective-permute-done((bf16[4,192,768]{2,1,0:T(8,128)(2,1)S(1)}, bf16[4,192,768]{2,1,0:T(8,128)(2,1)S(1)}, u32[]{:S(2)}, u32[]{:S(2)}) %collective-permute-start.13) | collective-permute-done | bytes 1179680 | tf_op jit(solution)/shard_map/ppermute | solution.py:39
  105.8 26.3 %collective-permute-done.8 = bf16[4,240,768]{2,1,0:T(8,128)(2,1)S(1)} collective-permute-done((bf16[4,240,768]{2,1,0:T(8,128)(2,1)S(1)}, bf16[4,240,768]{2,1,0:T(8,128)(2,1)S(1)}, u32[]{:S(2)}, u32[]{:S(2)}) %collective-permute-start.8) | collective-permute-done | bytes 1474592 | tf_op jit(solution)/shard_map/ppermute | solution.py:39
  150.2 6.5 copy.148
  156.8 8.2 %fusion.15 = bf16[1024,2304]{0,1:T(8,128)(2,1)} fusion(bf16[768,2304]{0,1:T(8,128)(2,1)S(1)} %bitcast.375, bf16[1024,768]{1,0:T(8,128)(2,1)} %bitcast.434, f32[2304]{0:T(1024)S(1)} %pad_maximum_fusion.9), kind=kOutput, calls=%fused_computation.45 | convolution fusion | flops 3628597248 | bytes 9839616 | tf_op jit(solution)/shard_map/dot_general | solution.py:73
  165.0 8.8 %reshape.454 = bf16[2,512,3,12,64]{1,0,4,3,2:T(2,128)(2,1)} reshape(bf16[1024,2304]{0,1:T(8,128)(2,1)} %fusion.15) | data formatting | bytes 9437184 | tf_op jit(solution)/shard_map/reshape | solution.py:223
  178.8 10.5 %fusion.14 = (f32[2,12,512]{2,1,0:T(8,128)S(1)}, f32[2,12,512,512]{2,3,1,0:T(8,128)}) fusion(pred[2,512,512]{1,2,0:T(8,128)(4,1)S(1)} %copy-done.9, bf16[2,512,1,12,64]{1,0,4,3,2:T(2,128)(2,1)S(1)} %get-tuple-element.141, bf16[2,512,1,12,64]{1,0,4,3,2:T(2,128)(2,1)S(1)} %get-tuple-element.140), kind=kOutput, calls=%fused_computation.38 | convolution fusion | flops 824168448 | bytes 28884992 | tf_op jit(solution)/shard_map/bqhd,bkhd->bhqk/dot_general | solution.py:112
  189.3 11.4 %fusion.2 = f32[2,12,512]{2,1,0:T(8,128)S(1)} fusion(f32[2,12,512]{2,1,0:T(8,128)S(1)} %get-tuple-element.198, f32[2,12,512,512]{2,3,1,0:T(8,128)} %get-tuple-element.199, pred[2,512,512]{1,2,0:T(8,128)(4,1)S(1)} %copy-done.9), kind=kLoop, calls=%fused_computation.15 | loop fusion | flops 25153536 | bytes 25788416 | tf_op jit(solution)/shard_map/reduce_sum | solution.py:228
  200.7 11.8 %fusion.27 = bf16[2,512,12,64]{1,3,2,0:T(8,128)(2,1)S(1)} fusion(f32[2,12,512]{2,1,0:T(8,128)S(1)} %fusion.2, f32[2,12,512]{2,1,0:T(8,128)S(1)} %get-tuple-element.198, f32[2,12,512,512]{2,3,1,0:T(8,128)} %get-tuple-element.199, pred[2,512,512]{1,2,0:T(8,128)(4,1)S(1)} %copy-done.9, bf16[2,512,1,12,64]{1,0,4,3,2:T(2,128)(2,1)S(1)} %get-tuple-element.139), kind=kOutput, calls=%fused_computation.93 | convolution fusion | flops 837550080 | bytes 28934144 | tf_op jit(solution)/shard_map/bhqk,bkhd->bqhd/dot_general | solution.py:231
  218.4 5.6 gather_fusion.4
  232.7 6.3 gather_fusion.1
  245.5 6.6 copy.156
  256.1 37.5 %multiply_convert_fusion.1 = (bf16[1024,3072]{1,0:T(8,128)(2,1)S(1)}, f32[1024,3072]{1,0:T(8,128)}, f32[1024,3072]{1,0:T(8,128)}) fusion(f32[3072]{0:T(1024)S(1)} %copy-done.55, bf16[768,3072]{0,1:T(8,128)(2,1)S(1)} %bitcast.388, f32[1024,768]{1,0:T(8,128)S(1)} %get-tuple-element.201, f32[768]{0:T(1024)S(1)} %copy-done.65, f32[768]{0:T(1024)S(1)} %get-tuple-element.115, ...), kind=kOutput, calls=%fused_computation.22 | convolution fusion | flops 5043388416 | bytes 39348224 | tf_op jit(solution)/shard_map/dot_general | solution.py:73
  335.1 7.3 %convolution_convert_fusion = bf16[3072,768]{1,0:T(8,128)(2,1)} fusion(bf16[1024,3072]{1,0:T(8,128)(2,1)S(1)} %bitcast.438, f32[1024,768]{1,0:T(8,128)S(1)} %get-tuple-element.128), kind=kOutput, calls=%fused_computation.42 | convolution fusion | flops 4834983936 | bytes 14155776 | tf_op jit(solution)/shard_map/dot_general | solution.py:77
  342.4 19.4 %fusion.117 = (bf16[3072]{0:T(1024)(128)(2,1)}, bf16[1024,3072]{1,0:T(8,128)(2,1)}) fusion(f32[1024,3072]{1,0:T(8,128)} %get-tuple-element.138, bf16[3072,768]{1,0:T(8,128)(2,1)} %bitcast.383, f32[1024,768]{1,0:T(8,128)} %copy-done.26, f32[1024,3072]{1,0:T(8,128)} %get-tuple-element.202, f32[3072]{0:T(1024)S(1)} %copy-done.55), kind=kOutput, calls=%fused_computation.328 | convolution fusion | flops 4882953216 | bytes 39340032 | tf_op jit(solution)/shard_map/dot_general | solution.py:83
  361.8 10.6 %multiply_reduce_fusion.1 = (bf16[768]{0:T(1024)(128)(2,1)}, f32[1024]{0:T(1024)S(1)}, f32[1024]{0:T(1024)S(1)}, bf16[768]{0:T(1024)(128)(2,1)}, f32[1024,768]{1,0:T(8,128)S(1)}) fusion(f32[1024,768]{1,0:T(8,128)S(1)} %copy-done.13, f32[1024]{0:T(1024)S(1)} %add_rsqrt_fusion.1, f32[1024]{0:T(1024)S(1)} %broadcast_multiply_fusion.5, ...), kind=kOutput, calls=%fused_computation.60 | convolution fusion | flops 4839698432 | bytes 20469760 | tf_op jit(solution)/shard_map/dot_general | solution.py:83
  372.4 8.2 %convolution_convert_fusion.1 = bf16[768,3072]{1,0:T(8,128)(2,1)} fusion(bf16[1024,3072]{1,0:T(8,128)(2,1)S(1)} %copy-done.72, f32[1024,768]{1,0:T(8,128)S(1)} %copy-done.13, f32[768]{0:T(1024)S(1)} %copy-done.65, f32[768]{0:T(1024)S(1)} %get-tuple-element.115, f32[1024]{0:T(1024)S(1)} %add_rsqrt_fusion.1, f32[1024]{0:T(1024)S(1)} %broadcast_multiply_fusion.5), kind=kOutput, calls=%fused_computation.43 | convolution fusion | flops 4838129664 | bytes 14170112 | tf_op jit(solution)/shard_map/dot_general | solution.py:77
  391.3 12.7 %fusion.22 = bf16[2,512,1,12,64]{1,4,3,0,2:T(8,128)(2,1)} fusion(f32[2,12,512]{2,1,0:T(8,128)S(1)} %copy-done.47, f32[2,12,512,512]{2,3,1,0:T(8,128)} %get-tuple-element.199, pred[2,512,512]{1,2,0:T(8,128)(4,1)S(1)} %copy-done.10, bf16[2,512,12,64]{1,0,3,2:T(2,128)(2,1)} %reshape.465), kind=kOutput, calls=%fused_computation.90 | convolution fusion | flops 831258624 | bytes 28884992 | tf_op jit(solution)/shard_map/bhqk,bqhd->bkhd/dot_general | solution.py:319
  404.0 18.2 %multiply_reduce_fusion = (f32[2,12,512]{2,1,0:T(8,128)S(1)}, f32[2,12,512,512]{2,3,1,0:T(8,128)}) fusion(f32[2,12,512]{2,1,0:T(8,128)S(1)} %copy-done.47, f32[2,12,512,512]{2,3,1,0:T(8,128)} %get-tuple-element.199, pred[2,512,512]{1,2,0:T(8,128)(4,1)S(1)} %copy-done.10, bf16[2,512,1,12,64]{1,0,4,3,2:T(2,128)(2,1)S(1)} %copy-done.15, ...), kind=kOutput, calls=%fused_computation.10 | convolution fusion | flops 836751360 | bytes 54099968 | tf_op jit(solution)/shard_map/bqhd,bkhd->bhqk/dot_general | solution.py:325
  422.3 21.5 %multiply_convert_fusion = bf16[2,12,512,512]{2,3,1,0:T(8,128)(2,1)} fusion(f32[2,12,512,512]{2,3,1,0:T(8,128)} %get-tuple-element.208, f32[2,12,512]{2,1,0:T(8,128)S(1)} %get-tuple-element.207, f32[2,12,512]{2,1,0:T(8,128)S(1)} %copy-done.47, f32[2,12,512,512]{2,3,1,0:T(8,128)} %get-tuple-element.199, pred[2,512,512]{1,2,0:T(8,128)(4,1)S(1)} %copy-done.10), kind=kLoop, calls=%fused_computation.9 | loop fusion | flops 37748736 | bytes 63537152 | tf_op jit(solution)/shard_map/convert_element_type | solution.py:329
  443.7 9.8 %fusion.26 = bf16[2,512,1,12,64]{1,4,3,0,2:T(8,128)(2,1)} fusion(bf16[2,12,512,512]{2,3,1,0:T(8,128)(2,1)} %multiply_convert_fusion, bf16[2,512,1,12,64]{1,0,4,3,2:T(2,128)(2,1)S(1)} %copy-done.6), kind=kOutput, calls=%fused_computation.92 | convolution fusion | flops 806879232 | bytes 15728640 | tf_op jit(solution)/shard_map/bhqk,bqhd->bkhd/dot_general | solution.py:335
  453.6 8.0 %fusion.25 = bf16[2,512,1,12,64]{1,4,3,0,2:T(8,128)(2,1)} fusion(bf16[2,12,512,512]{2,3,1,0:T(8,128)(2,1)} %multiply_convert_fusion, bf16[2,512,1,12,64]{1,0,4,3,2:T(2,128)(2,1)S(1)} %copy-done.1), kind=kOutput, calls=%fused_computation.91 | convolution fusion | flops 806879232 | bytes 15728640 | tf_op jit(solution)/shard_map/bhqk,bkhd->bqhd/dot_general | solution.py:331
  470.0 5.5 gather_fusion.5
  492.1 9.3 %copy.172 = bf16[2,512,3,12,64]{1,0,4,3,2:T(2,128)(2,1)} copy(bf16[2,512,3,12,64]{1,4,3,0,2:T(8,128)(2,1)} %get-tuple-element.132) | data formatting | bytes 9437184 | tf_op jit(solution)/shard_map/stack | solution.py:339
  529.4 8.5 %reshape_reshape.12 = bf16[3,16,48,768]{3,2,1,0:T(8,128)(2,1)S(1)} reshape(bf16[3,768,3,256]{3,2,1,0:T(4,128)(2,1)} %bitcast.374) | data formatting | bytes 7077888 | tf_op jit(solution)/shard_map/reshape;reshape | solution.py:283
  555.4 21.9 %collective-permute-done.27 = bf16[4,192,768]{2,1,0:T(8,128)(2,1)S(1)} collective-permute-done((bf16[4,192,768]{2,1,0:T(8,128)(2,1)S(1)}, bf16[4,192,768]{2,1,0:T(8,128)(2,1)S(1)}, u32[]{:S(2)}, u32[]{:S(2)}) %collective-permute-start.27) | collective-permute-done | bytes 1179680 | tf_op jit(solution)/shard_map/ppermute | solution.py:39
  581.3 21.3 %collective-permute-done.32 = bf16[4,192,768]{2,1,0:T(8,128)(2,1)S(1)} collective-permute-done((bf16[4,192,768]{2,1,0:T(8,128)(2,1)S(1)}, bf16[4,192,768]{2,1,0:T(8,128)(2,1)S(1)}, u32[]{:S(2)}, u32[]{:S(2)}) %collective-permute-start.32) | collective-permute-done | bytes 1179680 | tf_op jit(solution)/shard_map/ppermute | solution.py:39
  603.9 25.3 %collective-permute-done.22 = bf16[4,208,768]{2,1,0:T(8,128)(2,1)S(1)} collective-permute-done((bf16[4,208,768]{2,1,0:T(8,128)(2,1)S(1)}, bf16[4,208,768]{2,1,0:T(8,128)(2,1)S(1)}, u32[]{:S(2)}, u32[]{:S(2)}) %collective-permute-start.22) | collective-permute-done | bytes 1277984 | tf_op jit(solution)/shard_map/ppermute | solution.py:39
  641.0 31.0 %collective-permute-done.34 = bf16[192,768]{1,0:T(8,128)(2,1)S(1)} collective-permute-done((bf16[192,768]{1,0:T(8,128)(2,1)S(1)}, bf16[192,768]{1,0:T(8,128)(2,1)S(1)}, u32[]{:S(2)}, u32[]{:S(2)}) %collective-permute-start.34) | collective-permute-done | bytes 294944 | tf_op jit(solution)/shard_map/ppermute | solution.py:39
  673.6 10.4 %collective-permute-done.24 = bf16[208,768]{1,0:T(8,128)(2,1)S(1)} collective-permute-done((bf16[208,768]{1,0:T(8,128)(2,1)S(1)}, bf16[208,768]{1,0:T(8,128)(2,1)S(1)}, u32[]{:S(2)}, u32[]{:S(2)}) %collective-permute-start.24) | collective-permute-done | bytes 319520 | tf_op jit(solution)/shard_map/ppermute | solution.py:39
  704.7 8.1 %convolution_add_fusion.1 = f32[1024,768]{1,0:T(8,128)} fusion(f32[1024,768]{1,0:T(8,128)} %copy-done.11, bf16[1024,2304]{0,1:T(8,128)(2,1)} %bitcast.363, bf16[768,2304]{0,1:T(8,128)(2,1)S(1)} %bitcast.376), kind=kOutput, calls=%fused_computation.82 | convolution fusion | flops 3624665088 | bytes 14548992 | tf_op jit(solution)/shard_map/dot_general | solution.py:83
  (431 shorter events, 273.8 us)
Async XLA Ops:
  2.6 57.7 %collective-permute-start.12 = (bf16[192,768]{1,0:T(8,128)(2,1)}, bf16[192,768]{1,0:T(8,128)(2,1)S(1)}, u32[]{:S(2)}, u32[]{:S(2)}) collective-permute-start(bf16[192,768]{1,0:T(8,128)(2,1)} %bitcast_convert_fusion), channel_id=1, source_target_pairs={{0,12},{1,13},{2,14},{3,15},{4,8},{5,9},{6,10},{7,11},{8,4},{9,5},... | collective-permute-start | bytes 884744 | tf_op jit(solution)/shard_map/ppermute | solution.py:39
  7.6 55.6 %collective-permute-start.11 = (bf16[192,768]{1,0:T(8,128)(2,1)}, bf16[192,768]{1,0:T(8,128)(2,1)S(1)}, u32[]{:S(2)}, u32[]{:S(2)}) collective-permute-start(bf16[192,768]{1,0:T(8,128)(2,1)} %bitcast_convert_fusion), channel_id=1, source_target_pairs={{0,8},{1,9},{2,10},{3,11},{4,12},{5,13},{6,14},{7,15},{8,0},{9,1},... | collective-permute-start | bytes 884744 | tf_op jit(solution)/shard_map/ppermute | solution.py:39
  11.5 38.2 %collective-permute-start.1 = (bf16[160,768]{1,0:T(8,128)(2,1)}, bf16[160,768]{1,0:T(8,128)(2,1)S(1)}, u32[]{:S(2)}, u32[]{:S(2)}) collective-permute-start(bf16[160,768]{1,0:T(8,128)(2,1)} %get-tuple-element.188), channel_id=1, source_target_pairs={{0,8},{1,9},{2,10},{3,11},{4,12},{5,13},{6,14},{7,15},{8,0},{9,1},... | collective-permute-start | bytes 737288 | tf_op jit(solution)/shard_map/ppermute | solution.py:39
  14.4 35.3 %collective-permute-start = (bf16[160,768]{1,0:T(8,128)(2,1)}, bf16[160,768]{1,0:T(8,128)(2,1)S(1)}, u32[]{:S(2)}, u32[]{:S(2)}) collective-permute-start(bf16[160,768]{1,0:T(8,128)(2,1)} %get-tuple-element.188), channel_id=1, source_target_pairs={{0,4},{1,5},{2,6},{3,7},{4,0},{5,1},{6,2},{7,3},{8,12},{9,13},{10,... | collective-permute-start | bytes 737288 | tf_op jit(solution)/shard_map/ppermute | solution.py:39
  14.4 38.6 %collective-permute-start.2 = (bf16[160,768]{1,0:T(8,128)(2,1)}, bf16[160,768]{1,0:T(8,128)(2,1)S(1)}, u32[]{:S(2)}, u32[]{:S(2)}) collective-permute-start(bf16[160,768]{1,0:T(8,128)(2,1)} %get-tuple-element.188), channel_id=1, source_target_pairs={{0,12},{1,13},{2,14},{3,15},{4,8},{5,9},{6,10},{7,11},{8,4},{9,5},... | collective-permute-start | bytes 737288 | tf_op jit(solution)/shard_map/ppermute | solution.py:39
  49.7 17.7 %collective-permute-start.10 = (bf16[192,768]{1,0:T(8,128)(2,1)}, bf16[192,768]{1,0:T(8,128)(2,1)S(1)}, u32[]{:S(2)}, u32[]{:S(2)}) collective-permute-start(bf16[192,768]{1,0:T(8,128)(2,1)} %bitcast_convert_fusion), channel_id=1, source_target_pairs={{0,4},{1,5},{2,6},{3,7},{4,0},{5,1},{6,2},{7,3},{8,12},{9,13},{10,... | collective-permute-start | bytes 884744 | tf_op jit(solution)/shard_map/ppermute | solution.py:39
  49.8 30.6 %collective-permute-start.6 = (bf16[240,768]{1,0:T(8,128)(2,1)}, bf16[240,768]{1,0:T(8,128)(2,1)S(1)}, u32[]{:S(2)}, u32[]{:S(2)}) collective-permute-start(bf16[240,768]{1,0:T(8,128)(2,1)} %get-tuple-element.172), channel_id=1, source_target_pairs={{0,8},{1,9},{2,10},{3,11},{4,12},{5,13},{6,14},{7,15},{8,0},{9,1},... | collective-permute-start | bytes 1105928 | tf_op jit(solution)/shard_map/ppermute | solution.py:39
  54.1 24.9 %collective-permute-start.3 = (bf16[4,160,768]{2,1,0:T(8,128)(2,1)}, bf16[4,160,768]{2,1,0:T(8,128)(2,1)S(1)}, u32[]{:S(2)}, u32[]{:S(2)}) collective-permute-start(bf16[4,160,768]{2,1,0:T(8,128)(2,1)} %pad_maximum_fusion.4), channel_id=1, source_target_pairs={{0,2},{1,3},{2,0},{3,1},{4,6},{5,7},{6,4},{7,5},{8,10},{9,11},{10,... | collective-permute-start | bytes 2949128 | tf_op jit(solution)/shard_map/ppermute | solution.py:39
  60.3 21.6 %collective-permute-start.5 = (bf16[240,768]{1,0:T(8,128)(2,1)}, bf16[240,768]{1,0:T(8,128)(2,1)S(1)}, u32[]{:S(2)}, u32[]{:S(2)}) collective-permute-start(bf16[240,768]{1,0:T(8,128)(2,1)} %get-tuple-element.172), channel_id=1, source_target_pairs={{0,4},{1,5},{2,6},{3,7},{4,0},{5,1},{6,2},{7,3},{8,12},{9,13},{10,... | collective-permute-start | bytes 1105928 | tf_op jit(solution)/shard_map/ppermute | solution.py:39
  63.2 18.7 %collective-permute-start.7 = (bf16[240,768]{1,0:T(8,128)(2,1)}, bf16[240,768]{1,0:T(8,128)(2,1)S(1)}, u32[]{:S(2)}, u32[]{:S(2)}) collective-permute-start(bf16[240,768]{1,0:T(8,128)(2,1)} %get-tuple-element.172), channel_id=1, source_target_pairs={{0,12},{1,13},{2,14},{3,15},{4,8},{5,9},{6,10},{7,11},{8,4},{9,5},... | collective-permute-start | bytes 1105928 | tf_op jit(solution)/shard_map/ppermute | solution.py:39
  67.6 36.6 %collective-permute-start.13 = (bf16[4,192,768]{2,1,0:T(8,128)(2,1)S(1)}, bf16[4,192,768]{2,1,0:T(8,128)(2,1)S(1)}, u32[]{:S(2)}, u32[]{:S(2)}) collective-permute-start(bf16[4,192,768]{2,1,0:T(8,128)(2,1)S(1)} %pad_maximum_fusion.3), channel_id=1, source_target_pairs={{0,2},{1,3},{2,0},{3,1},{4,6},{5,7},{6,4},{7,5},{8,10},{9,11},{10,... | collective-permute-start | bytes 3538952 | tf_op jit(solution)/shard_map/ppermute | solution.py:39
  80.4 53.5 %collective-permute-start.4 = (bf16[8,160,768]{2,1,0:T(8,128)(2,1)}, bf16[8,160,768]{2,1,0:T(8,128)(2,1)S(1)}, u32[]{:S(2)}, u32[]{:S(2)}) collective-permute-start(bf16[8,160,768]{2,1,0:T(8,128)(2,1)} %get-tuple-element.158), channel_id=1, source_target_pairs={{0,1},{1,0},{2,3},{3,2},{4,5},{5,4},{6,7},{7,6},{8,9},{9,8},{10,11... | collective-permute-start | bytes 5898248 | tf_op jit(solution)/shard_map/ppermute | solution.py:39
  82.1 50.0 %collective-permute-start.8 = (bf16[4,240,768]{2,1,0:T(8,128)(2,1)S(1)}, bf16[4,240,768]{2,1,0:T(8,128)(2,1)S(1)}, u32[]{:S(2)}, u32[]{:S(2)}) collective-permute-start(bf16[4,240,768]{2,1,0:T(8,128)(2,1)S(1)} %pad_maximum_fusion.2), channel_id=1, source_target_pairs={{0,2},{1,3},{2,0},{3,1},{4,6},{5,7},{6,4},{7,5},{8,10},{9,11},{10,... | collective-permute-start | bytes 4423688 | tf_op jit(solution)/shard_map/ppermute | solution.py:39
  105.8 109.4 %collective-permute-start.14 = (bf16[8,192,768]{2,1,0:T(8,128)(2,1)}, bf16[8,192,768]{2,1,0:T(8,128)(2,1)}, u32[]{:S(2)}, u32[]{:S(2)}) collective-permute-start(bf16[8,192,768]{2,1,0:T(8,128)(2,1)} %get-tuple-element.156), channel_id=1, source_target_pairs={{0,1},{1,0},{2,3},{3,2},{4,5},{5,4},{6,7},{7,6},{8,9},{9,8},{10,11... | collective-permute-start | bytes 7077896 | tf_op jit(solution)/shard_map/ppermute | solution.py:39
  133.8 95.2 %collective-permute-start.9 = (bf16[8,240,768]{2,1,0:T(8,128)(2,1)}, bf16[8,240,768]{2,1,0:T(8,128)(2,1)}, u32[]{:S(2)}, u32[]{:S(2)}) collective-permute-start(bf16[8,240,768]{2,1,0:T(8,128)(2,1)} %get-tuple-element.142), channel_id=1, source_target_pairs={{0,1},{1,0},{2,3},{3,2},{4,5},{5,4},{6,7},{7,6},{8,9},{9,8},{10,11... | collective-permute-start | bytes 8847368 | tf_op jit(solution)/shard_map/ppermute | solution.py:39
  308.0 6.6 collective-permute-start.17
  488.2 57.0 %collective-permute-start.26 = (bf16[8,192,768]{2,1,0:T(8,128)(2,1)}, bf16[8,192,768]{2,1,0:T(8,128)(2,1)}, u32[]{:S(2)}, u32[]{:S(2)}) collective-permute-start(bf16[8,192,768]{2,1,0:T(8,128)(2,1)} %slice.284), channel_id=1, source_target_pairs={{0,1},{1,0},{2,3},{3,2},{4,5},{5,4},{6,7},{7,6},{8,9},{9,8},{10,11... | collective-permute-start | bytes 7077896 | tf_op jit(solution)/shard_map/ppermute | solution.py:39
  488.3 61.8 %collective-permute-start.31 = (bf16[8,192,768]{2,1,0:T(8,128)(2,1)}, bf16[8,192,768]{2,1,0:T(8,128)(2,1)}, u32[]{:S(2)}, u32[]{:S(2)}) collective-permute-start(bf16[8,192,768]{2,1,0:T(8,128)(2,1)} %slice.292), channel_id=1, source_target_pairs={{0,1},{1,0},{2,3},{3,2},{4,5},{5,4},{6,7},{7,6},{8,9},{9,8},{10,11... | collective-permute-start | bytes 7077896 | tf_op jit(solution)/shard_map/ppermute | solution.py:39
  545.0 8.1 %collective-permute-start.21 = (bf16[8,208,768]{2,1,0:T(8,128)(2,1)S(1)}, bf16[8,208,768]{2,1,0:T(8,128)(2,1)S(1)}, u32[]{:S(2)}, u32[]{:S(2)}) collective-permute-start(bf16[8,208,768]{2,1,0:T(8,128)(2,1)S(1)} %slice.274), channel_id=1, source_target_pairs={{0,1},{1,0},{2,3},{3,2},{4,5},{5,4},{6,7},{7,6},{8,9},{9,8},{10,11... | collective-permute-start | bytes 7667720 | tf_op jit(solution)/shard_map/ppermute | solution.py:39
  548.5 28.9 %collective-permute-start.27 = (bf16[4,192,768]{2,1,0:T(8,128)(2,1)S(1)}, bf16[4,192,768]{2,1,0:T(8,128)(2,1)S(1)}, u32[]{:S(2)}, u32[]{:S(2)}) collective-permute-start(bf16[4,192,768]{2,1,0:T(8,128)(2,1)S(1)} %slice.286), channel_id=1, source_target_pairs={{0,2},{1,3},{2,0},{3,1},{4,6},{5,7},{6,4},{7,5},{8,10},{9,11},{10,... | collective-permute-start | bytes 3538952 | tf_op jit(solution)/shard_map/ppermute | solution.py:39
  552.4 50.2 %collective-permute-start.32 = (bf16[4,192,768]{2,1,0:T(8,128)(2,1)S(1)}, bf16[4,192,768]{2,1,0:T(8,128)(2,1)S(1)}, u32[]{:S(2)}, u32[]{:S(2)}) collective-permute-start(bf16[4,192,768]{2,1,0:T(8,128)(2,1)S(1)} %slice.294), channel_id=1, source_target_pairs={{0,2},{1,3},{2,0},{3,1},{4,6},{5,7},{6,4},{7,5},{8,10},{9,11},{10,... | collective-permute-start | bytes 3538952 | tf_op jit(solution)/shard_map/ppermute | solution.py:39
  553.9 75.3 %collective-permute-start.22 = (bf16[4,208,768]{2,1,0:T(8,128)(2,1)S(1)}, bf16[4,208,768]{2,1,0:T(8,128)(2,1)S(1)}, u32[]{:S(2)}, u32[]{:S(2)}) collective-permute-start(bf16[4,208,768]{2,1,0:T(8,128)(2,1)S(1)} %slice.276), channel_id=1, source_target_pairs={{0,2},{1,3},{2,0},{3,1},{4,6},{5,7},{6,4},{7,5},{8,10},{9,11},{10,... | collective-permute-start | bytes 3833864 | tf_op jit(solution)/shard_map/ppermute | solution.py:39
  577.7 54.1 %collective-permute-start.28 = (bf16[192,768]{1,0:T(8,128)(2,1)S(1)}, bf16[192,768]{1,0:T(8,128)(2,1)S(1)}, u32[]{:S(2)}, u32[]{:S(2)}) collective-permute-start(bf16[192,768]{1,0:T(8,128)(2,1)S(1)} %get-tuple-element.153), channel_id=1, source_target_pairs={{0,4},{1,5},{2,6},{3,7},{4,0},{5,1},{6,2},{7,3},{8,12},{9,13},{10,... | collective-permute-start | bytes 884744 | tf_op jit(solution)/shard_map/ppermute | solution.py:39
  578.6 53.4 %collective-permute-start.30 = (bf16[192,768]{1,0:T(8,128)(2,1)S(1)}, bf16[192,768]{1,0:T(8,128)(2,1)S(1)}, u32[]{:S(2)}, u32[]{:S(2)}) collective-permute-start(bf16[192,768]{1,0:T(8,128)(2,1)S(1)} %get-tuple-element.154), channel_id=1, source_target_pairs={{0,12},{1,13},{2,14},{3,15},{4,8},{5,9},{6,10},{7,11},{8,4},{9,5},... | collective-permute-start | bytes 884744 | tf_op jit(solution)/shard_map/ppermute | solution.py:39
  580.6 53.6 %collective-permute-start.29 = (bf16[192,768]{1,0:T(8,128)(2,1)S(1)}, bf16[192,768]{1,0:T(8,128)(2,1)S(1)}, u32[]{:S(2)}, u32[]{:S(2)}) collective-permute-start(bf16[192,768]{1,0:T(8,128)(2,1)S(1)} %get-tuple-element.155), channel_id=1, source_target_pairs={{0,8},{1,9},{2,10},{3,11},{4,12},{5,13},{6,14},{7,15},{8,0},{9,1},... | collective-permute-start | bytes 884744 | tf_op jit(solution)/shard_map/ppermute | solution.py:39
  603.0 33.5 %collective-permute-start.33 = (bf16[192,768]{1,0:T(8,128)(2,1)S(1)}, bf16[192,768]{1,0:T(8,128)(2,1)S(1)}, u32[]{:S(2)}, u32[]{:S(2)}) collective-permute-start(bf16[192,768]{1,0:T(8,128)(2,1)S(1)} %get-tuple-element.150), channel_id=1, source_target_pairs={{0,4},{1,5},{2,6},{3,7},{4,0},{5,1},{6,2},{7,3},{8,12},{9,13},{10,... | collective-permute-start | bytes 884744 | tf_op jit(solution)/shard_map/ppermute | solution.py:39
  629.2 11.8 %collective-permute-start.35 = (bf16[192,768]{1,0:T(8,128)(2,1)S(1)}, bf16[192,768]{1,0:T(8,128)(2,1)S(1)}, u32[]{:S(2)}, u32[]{:S(2)}) collective-permute-start(bf16[192,768]{1,0:T(8,128)(2,1)S(1)} %get-tuple-element.151), channel_id=1, source_target_pairs={{0,12},{1,13},{2,14},{3,15},{4,8},{5,9},{6,10},{7,11},{8,4},{9,5},... | collective-permute-start | bytes 884744 | tf_op jit(solution)/shard_map/ppermute | solution.py:39
  631.9 40.1 %collective-permute-start.34 = (bf16[192,768]{1,0:T(8,128)(2,1)S(1)}, bf16[192,768]{1,0:T(8,128)(2,1)S(1)}, u32[]{:S(2)}, u32[]{:S(2)}) collective-permute-start(bf16[192,768]{1,0:T(8,128)(2,1)S(1)} %get-tuple-element.152), channel_id=1, source_target_pairs={{0,8},{1,9},{2,10},{3,11},{4,12},{5,13},{6,14},{7,15},{8,0},{9,1},... | collective-permute-start | bytes 884744 | tf_op jit(solution)/shard_map/ppermute | solution.py:39
  632.0 41.5 %collective-permute-start.23 = (bf16[208,768]{1,0:T(8,128)(2,1)S(1)}, bf16[208,768]{1,0:T(8,128)(2,1)S(1)}, u32[]{:S(2)}, u32[]{:S(2)}) collective-permute-start(bf16[208,768]{1,0:T(8,128)(2,1)S(1)} %get-tuple-element.144), channel_id=1, source_target_pairs={{0,4},{1,5},{2,6},{3,7},{4,0},{5,1},{6,2},{7,3},{8,12},{9,13},{10,... | collective-permute-start | bytes 958472 | tf_op jit(solution)/shard_map/ppermute | solution.py:39
  634.2 39.4 %collective-permute-start.25 = (bf16[208,768]{1,0:T(8,128)(2,1)S(1)}, bf16[208,768]{1,0:T(8,128)(2,1)S(1)}, u32[]{:S(2)}, u32[]{:S(2)}) collective-permute-start(bf16[208,768]{1,0:T(8,128)(2,1)S(1)} %get-tuple-element.145), channel_id=1, source_target_pairs={{0,12},{1,13},{2,14},{3,15},{4,8},{5,9},{6,10},{7,11},{8,4},{9,5},... | collective-permute-start | bytes 958472 | tf_op jit(solution)/shard_map/ppermute | solution.py:39
  636.5 47.5 %collective-permute-start.24 = (bf16[208,768]{1,0:T(8,128)(2,1)S(1)}, bf16[208,768]{1,0:T(8,128)(2,1)S(1)}, u32[]{:S(2)}, u32[]{:S(2)}) collective-permute-start(bf16[208,768]{1,0:T(8,128)(2,1)S(1)} %get-tuple-element.146), channel_id=1, source_target_pairs={{0,8},{1,9},{2,10},{3,11},{4,12},{5,13},{6,14},{7,15},{8,0},{9,1},... | collective-permute-start | bytes 958472 | tf_op jit(solution)/shard_map/ppermute | solution.py:39
  703.2 9.7 %collective-permute-start.40 = (f32[8,128]{1,0:T(8,128)S(1)}, f32[8,128]{1,0:T(8,128)S(1)}, u32[]{:S(2)}, u32[]{:S(2)}) collective-permute-start(f32[8,128]{1,0:T(8,128)S(1)} %add.383), channel_id=1, source_target_pairs={{0,16},{16,0},{1,17},{17,1},{2,18},{18,2},{3,19},{19,3},{4,20},{20... | collective-permute-start | bytes 12296 | tf_op jit(solution)/shard_map/ppermute | solution.py:43
  (93 other events, 1266.1 us)

commit v2 on v1

v2 whole, which is shorter than its diff:
```python
from functools import partial

import jax
import jax.numpy as jnp
from jax import lax
from jax.experimental import pallas as pl
from jax.experimental.pallas import tpu as pltpu
from jax.sharding import PartitionSpec as P

D = 768
FF = 3072
H = 12
HD = 64
L = 512
SEGS = 8
MB = 2
STEP = 5
HG = 3
PIECES = 16
PIECE_ROWS = D // PIECES

norm_eps = 1e-05
attention_scale = 0.125
score_scale = 0.0625
contrast_weight = 16.0
clip_norm = 1.0
beta_first = 0.9
beta_second = 0.999
adam_eps = 1e-08
weight_decay = 0.01
matrix_rate = 0.05
vector_rate = 0.5
masked_score = -1e30

low_type = jnp.bfloat16
highest = lax.Precision.HIGHEST


def swapped(value, mask):
    pairs = [(i, i ^ mask) for i in range(lax.axis_size("dp"))]
    return lax.ppermute(value, "dp", pairs)


def tower_swapped(value):
    return lax.ppermute(value, "tower", [(0, 1), (1, 0)])


def relative_of(place):
    return ((place & 1) << 3) | ((place & 2) << 1) | ((place & 4) >> 1) | (place >> 3)


def gather_pieces(own):
    pieces = own[None]
    for mask in (8, 4, 2, 1):
        pieces = jnp.concatenate([pieces, swapped(pieces, mask)])
    return pieces


def added(first, second):
    return first.astype(jnp.float32) + second.astype(jnp.float32)


def rows_dot(first_op, second_op):
    return jnp.dot(first_op, second_op, preferred_element_type=jnp.float32)


def contract_rows(first_op, second_op):
    return lax.dot_general(
        first_op, second_op, (((0,), (0,)), ((), ())), preferred_element_type=jnp.float32
    )


def contract_cols(first_op, second_op):
    return lax.dot_general(
        first_op, second_op, (((1,), (1,)), ((), ())), preferred_element_type=jnp.float32
    )


def layer_stats(values):
    centred = values - jnp.mean(values, axis=-1, keepdims=True)
    inverse = lax.rsqrt(jnp.mean(centred * centred, axis=-1, keepdims=True) + norm_eps)
    return (centred * inverse, inverse)


def norm_back(upstream, normed, inverse, gain_row):
    gained = upstream * gain_row
    return inverse * (
        gained
        - jnp.mean(gained, axis=-1, keepdims=True)
        - normed * jnp.mean(gained * normed, axis=-1, keepdims=True)
    )


def column_sum(values):
    return jnp.sum(values.astype(jnp.float32), axis=0, keepdims=True)


def gelu_parts(pre):
    size = jnp.abs(pre) * 0.7071067811865476
    inner = 1.0 / (1.0 + 0.3275911 * size)
    series = 1.061405429 * inner - 1.453152027
    series = series * inner + 1.421413741
    series = series * inner - 0.284496736
    series = (series * inner + 0.254829592) * inner
    bell = jnp.exp(-size * size)
    half_tail = 0.5 * series * bell
    cumulative = jnp.where(pre >= 0.0, 1.0 - half_tail, half_tail)
    return (pre * cumulative, cumulative + pre * (bell * 0.3989422804014327))


ROWS = MB * L
QCOLS = D // HG
HEADS = H // HG
log2e = 1.4426950408889634
any_space = pl.BlockSpec(memory_space=pl.ANY)
scalar_space = pl.BlockSpec(memory_space=pltpu.SMEM)
vmem_space = pl.BlockSpec(memory_space=pltpu.VMEM)


def params(megabytes):
    return pltpu.CompilerParams(vmem_limit_bytes=megabytes * 1024 * 1024)


def cost(flops, moved, exps=0):
    return pl.CostEstimate(flops=int(flops), bytes_accessed=int(moved), transcendentals=int(exps))


def start_pieces(me, near, far, row, count, target, sem):
    for place in range(PIECES):
        held = near if place < 8 else far
        at = pl.multiple_of((me ^ relative_of(place)) * count, 16)
        pltpu.make_async_copy(
            held.at[place % 8, pl.ds(row, count), :], target.at[pl.ds(at, count), :], sem
        ).start()


def start_owners(me, source, count, keep, send, row, sem):
    for place in range(PIECES):
        held = keep if place < 8 else send
        at = pl.multiple_of((me ^ relative_of(place)) * count, 16)
        pltpu.make_async_copy(
            source.at[pl.ds(at, count), :], held.at[place % 8, pl.ds(row, count), :], sem
        ).start()


def wait_bytes(whole, sem):
    pltpu.make_async_copy(whole, whole, sem).wait()


def attention_kernel(
    me_ref, near, far, x_ref, seg_col, seg_row, bias_ref, mixed_ref, ctx_ref, lse_ref, w, mask, sems
):
    hg, mb = pl.program_id(0), pl.program_id(1)
    me = me_ref[0]

    @pl.when((hg == 0) & (mb == 0))
    def _():
        for block in range(HG):
            start_pieces(
                me, near, far, block * PIECE_ROWS, PIECE_ROWS, w.at[block], sems.at[block]
            )

    @pl.when(hg == 0)
    def _():
        same = seg_col[...] == seg_row[...].reshape(1, L)
        mask[mb] = jnp.where(same, 0.0, masked_score)

    for block in range(HG):

        @pl.when((hg == block) & (mb == 0))
        def _():
            wait_bytes(w.at[block], sems.at[block])

    mixed = (rows_dot(x_ref[...], w[hg]) + bias_ref[...].reshape(1, D)).astype(low_type)
    mixed_ref[...] = mixed.reshape(mixed_ref.shape)
    outs, totals = [], []
    for head in range(HEADS):
        q = mixed[:, head * HD : (head + 1) * HD]
        k = mixed[:, QCOLS + head * HD : QCOLS + (head + 1) * HD]
        v = mixed[:, 2 * QCOLS + head * HD : 2 * QCOLS + (head + 1) * HD]
        parts, logs = [], []
        for first in range(0, L, 256):
            scores = contract_cols(q[first : first + 256], k) * (attention_scale * log2e)
            scores = scores + mask[mb, first : first + 256, :]
            largest = jnp.max(scores, axis=-1, keepdims=True)
            expo = jnp.exp2(scores - largest)
            summed = jnp.sum(expo, axis=-1, keepdims=True)
            probs = (expo * (1.0 / summed)).astype(low_type)
            parts.append(rows_dot(probs, v))
            logs.append(largest + jnp.log(summed) * log2e)
        outs.append(jnp.concatenate(parts, axis=0))
        totals.append(jnp.concatenate(logs, axis=0))
    ctx_ref[...] = jnp.concatenate(outs, axis=1).astype(low_type)
    lse_ref[...] = jnp.concatenate(totals, axis=1).reshape(lse_ref.shape)


def attention_forward(me, near, far, x_low, seg_col, seg_row, mixed_bias):
    count = near.shape[1]
    return pl.pallas_call(
        attention_kernel,
        grid=(HG, MB),
        in_specs=[
            scalar_space,
            any_space,
            any_space,
            pl.BlockSpec((L, D), lambda g, m: (m, 0)),
            pl.BlockSpec((L, 1), lambda g, m: (m, 0)),
            pl.BlockSpec((1, 1, L), lambda g, m: (m, 0, 0)),
            pl.BlockSpec((1, 1, D), lambda g, m: (g, 0, 0)),
        ],
        out_specs=[
            pl.BlockSpec((1, L, D), lambda g, m: (g, m, 0)),
            pl.BlockSpec((L, QCOLS), lambda g, m: (m, g)),
            pl.BlockSpec((1, L, HEADS), lambda g, m: (g * MB + m, 0, 0)),
        ],
        out_shape=[
            jax.ShapeDtypeStruct((HG, ROWS, D), low_type),
            jax.ShapeDtypeStruct((ROWS, D), low_type),
            jax.ShapeDtypeStruct((HG * MB, L, HEADS), jnp.float32),
        ],
        scratch_shapes=[
            pltpu.VMEM((HG, D, D), low_type),
            pltpu.VMEM((MB, L, L), jnp.float32),
            pltpu.SemaphoreType.DMA((HG,)),
        ],
        compiler_params=params(40),
        cost_estimate=cost(2 * ROWS * D * 3 * D + 8 * MB * H * L * L * HD, 12e6, MB * H * L * L),
        name="mixed_attention",
    )(me, near, far, x_low, seg_col, seg_row, mixed_bias)


def up_kernel(
    me_ref,
    near,
    far,
    ctx_hbm,
    x_hbm,
    vec,
    normed_hbm,
    inverse_ref,
    hidden_hbm,
    active_ref,
    slope_ref,
    out_w,
    up_w,
    ctx,
    x,
    normed,
    hidden,
    sems,
):
    step = pl.program_id(0)
    me = me_ref[0]
    ctx_in = pltpu.make_async_copy(ctx_hbm, ctx, sems.at[5])
    x_in = pltpu.make_async_copy(x_hbm, x, sems.at[6])
    normed_out = pltpu.make_async_copy(normed, normed_hbm, sems.at[7])
    hidden_out = pltpu.make_async_copy(hidden, hidden_hbm, sems.at[8])

    @pl.when(step == 0)
    def _():
        start_pieces(me, near, far, 0, PIECE_ROWS, out_w, sems.at[4])
        ctx_in.start()
        x_in.start()
        for block in range(4):
            start_pieces(
                me,
                near,
                far,
                (1 + block) * PIECE_ROWS,
                PIECE_ROWS,
                up_w.at[block],
                sems.at[block],
            )
        wait_bytes(out_w, sems.at[4])
        ctx_in.wait()
        x_in.wait()
        for first in range(0, ROWS, 256):
            part = slice(first, first + 256)
            branch = rows_dot(ctx[part, :], out_w[...]) + vec[2:3, :]
            n, inv = layer_stats(x[part, :].astype(jnp.float32) + branch)
            normed[part, :] = n
            inverse_ref[part, :] = inv
            hidden[part, :] = (n * vec[3:4, :] + vec[4:5, :]).astype(low_type)
        normed_out.start()
        hidden_out.start()

    for block in range(4):

        @pl.when(step == block)
        def _():
            wait_bytes(up_w.at[block], sems.at[block])

    bias = vec[pl.ds(5 + step, 1), :]
    for first in range(0, ROWS, 256):
        part = slice(first, first + 256)
        pre = rows_dot(hidden[part, :], up_w[step]) + bias
        active, slope = gelu_parts(pre)
        active_ref[part, :] = active.astype(low_type)
        slope_ref[part, :] = slope.astype(low_type)

    @pl.when(step == 3)
    def _():
        normed_out.wait()
        hidden_out.wait()


def up_forward(me, near, far, context, x_low, vec):
    return pl.pallas_call(
        up_kernel,
        grid=(4,),
        in_specs=[scalar_space, any_space, any_space, any_space, any_space, vmem_space],
        out_specs=[
            any_space,
            pl.BlockSpec((ROWS, 1), lambda s: (0, 0)),
            any_space,
            pl.BlockSpec((ROWS, D), lambda s: (0, s)),
            pl.BlockSpec((ROWS, D), lambda s: (0, s)),
        ],
        out_shape=[
            jax.ShapeDtypeStruct((ROWS, D), jnp.float32),
            jax.ShapeDtypeStruct((ROWS, 1), jnp.float32),
            jax.ShapeDtypeStruct((ROWS, D), low_type),
            jax.ShapeDtypeStruct((ROWS, FF), low_type),
            jax.ShapeDtypeStruct((ROWS, FF), low_type),
        ],
        scratch_shapes=[
            pltpu.VMEM((D, D), low_type),
            pltpu.VMEM((4, D, D), low_type),
            pltpu.VMEM((ROWS, D), low_type),
            pltpu.VMEM((ROWS, D), low_type),
            pltpu.VMEM((ROWS, D), jnp.float32),
            pltpu.VMEM((ROWS, D), low_type),
            pltpu.SemaphoreType.DMA((9,)),
        ],
        compiler_params=params(44),
        cost_estimate=cost(2 * ROWS * D * (FF + D), 24e6, 2 * ROWS * FF),
        name="out_up",
    )(me, near, far, context, x_low, vec)


def down_kernel(
    me_ref,
    near,
    far,
    active_hbm,
    normed_one_ref,
    vec,
    table_ref,
    normed_ref,
    inverse_ref,
    output_ref,
    cls_ref,
    w,
    active,
    sems,
):
    me = me_ref[0]
    start_pieces(me, near, far, 0, 4 * PIECE_ROWS, w, sems.at[0])
    copies = []
    for index in range(4):
        part = pl.ds(index * 256, 256)
        copies.append(
            pltpu.make_async_copy(active_hbm.at[part, :], active.at[part, :], sems.at[1 + index])
        )
        copies[-1].start()
    wait_bytes(w, sems.at[0])
    for index in range(4):
        copies[index].wait()
        part = slice(index * 256, (index + 1) * 256)
        ffn = rows_dot(active[part, :], w[...]) + vec[9:10, :]
        residual = normed_one_ref[part, :] * vec[3:4, :] + vec[4:5, :]
        n, inv = layer_stats(residual + ffn)
        normed_ref[part, :] = n
        inverse_ref[part, :] = inv
        output_ref[part, :] = (n * vec[10:11, :] + vec[11:12, :]).astype(low_type)
    cls_ref[...] = rows_dot(table_ref[...], output_ref[...]).astype(low_type)


def down_forward(me, near, far, active, normed_one, vec, table):
    return pl.pallas_call(
        down_kernel,
        in_specs=[scalar_space, any_space, any_space, any_space, vmem_space, vmem_space, vmem_space],
        out_specs=[vmem_space] * 4,
        out_shape=[
            jax.ShapeDtypeStruct((ROWS, D), jnp.float32),
            jax.ShapeDtypeStruct((ROWS, 1), jnp.float32),
            jax.ShapeDtypeStruct((ROWS, D), low_type),
            jax.ShapeDtypeStruct((MB * SEGS, D), low_type),
        ],
        scratch_shapes=[
            pltpu.VMEM((FF, D), low_type),
            pltpu.VMEM((ROWS, FF), low_type),
            pltpu.SemaphoreType.DMA((5,)),
        ],
        compiler_params=params(40),
        cost_estimate=cost(2 * ROWS * D * FF, 19e6),
        name="down",
    )(me, near, far, active, normed_one, vec, table)


def contrast_kernel(flag_ref, all_ref, positive_ref, ids_ref, grad_ref):
    passage_here = flag_ref[0] == 1
    for batch in range(MB):
        mine, theirs = all_ref[0, batch], all_ref[1, batch]
        queries = jnp.where(passage_here, theirs, mine)
        passages = jnp.where(passage_here, mine, theirs)
        contrast = contract_cols(queries, passages) * score_scale
        top = jnp.max(contrast, axis=-1, keepdims=True)
        expo = jnp.exp(contrast - top)
        probs = expo / jnp.sum(expo, axis=-1, keepdims=True)
        chosen = (positive_ref[batch] == ids_ref[...]).astype(jnp.float32)
        grad = (contrast_weight * (probs - chosen)).astype(low_type)
        for_query = rows_dot(grad[:16], passages) * score_scale
        for_query = for_query.astype(low_type).astype(jnp.float32)
        for_passage = contract_rows(grad, queries)[:16] * score_scale
        taken = jnp.where(passage_here, for_passage, for_query)
        grad_ref[batch * SEGS : (batch + 1) * SEGS, :] = taken[:SEGS]


def contrast_back(flag, everyone, cls_positives, cls_ids):
    return pl.pallas_call(
        contrast_kernel,
        in_specs=[scalar_space, vmem_space, vmem_space, vmem_space],
        out_specs=vmem_space,
        out_shape=jax.ShapeDtypeStruct((MB * SEGS, D), jnp.float32),
        compiler_params=params(48),
        name="contrast",
    )(flag, everyone, cls_positives, cls_ids)


def down_back_kernel(
    me_ref,
    token_grad,
    grad_cls,
    table3_ref,
    normed_ref,
    inverse_ref,
    vec,
    active_ref,
    residual_ref,
    low_ref,
    sums_ref,
    keep,
    send,
    low,
    staged,
    sem,
):
    step = pl.program_id(0)

    @pl.when(step == 0)
    def _():
        grads = grad_cls[...]
        upper = grads.astype(low_type)
        rest = grads - upper.astype(jnp.float32)
        middle = rest.astype(low_type)
        lower = (rest - middle.astype(jnp.float32)).astype(low_type)
        stacked = jnp.concatenate([upper, middle, lower], axis=0)
        gains = jnp.zeros((1, D), jnp.float32)
        shifts = jnp.zeros((1, D), jnp.float32)
        biases = jnp.zeros((1, D), jnp.float32)
        for first in range(0, ROWS, 256):
            part = slice(first, first + 256)
            upstream = token_grad[part, :] + contract_rows(table3_ref[:, part], stacked)
            n = normed_ref[part, :]
            gains = gains + column_sum(upstream * n)
            shifts = shifts + column_sum(upstream)
            grad = norm_back(upstream, n, inverse_ref[part, :], vec[10:11, :])
            residual_ref[part, :] = grad
            rounded = grad.astype(low_type)
            biases = biases + column_sum(rounded)
            low[part, :] = rounded
        low_ref[...] = low[...]
        sums_ref[...] = jnp.concatenate([biases, gains, shifts, jnp.zeros((5, D), jnp.float32)])

    at = pl.multiple_of(step * D, D)
    for first in range(0, D, 256):
        staged[pl.ds(at + first, 256), :] = contract_rows(
            active_ref[:, first : first + 256], low[...]
        ).astype(low_type)

    @pl.when(step == 3)
    def _():
        start_owners(me_ref[0], staged, 4 * PIECE_ROWS, keep, send, 0, sem)
        wait_bytes(staged, sem)


def down_back(me, token_grad, grad_cls, table3, normed, inverse, vec, active):
    half = jax.ShapeDtypeStruct((8, 4 * PIECE_ROWS, D), low_type)
    return pl.pallas_call(
        down_back_kernel,
        grid=(4,),
        in_specs=[scalar_space]
        + [vmem_space] * 6
        + [pl.BlockSpec((ROWS, D), lambda s: (0, s))],
        out_specs=[vmem_space] * 3 + [any_space] * 2,
        out_shape=[
            jax.ShapeDtypeStruct((ROWS, D), jnp.float32),
            jax.ShapeDtypeStruct((ROWS, D), low_type),
            jax.ShapeDtypeStruct((8, D), jnp.float32),
            half,
            half,
        ],
        scratch_shapes=[
            pltpu.VMEM((ROWS, D), low_type),
            pltpu.VMEM((FF, D), low_type),
            pltpu.SemaphoreType.DMA,
        ],
        compiler_params=params(48),
        cost_estimate=cost(2 * ROWS * D * FF, 25e6),
        name="down_back",
    )(me, token_grad, grad_cls, table3, normed, inverse, vec, active)


def up_back_kernel(
    me_ref,
    near_up,
    far_up,
    near_down,
    far_down,
    low_ref,
    slope_ref,
    hidden_ref,
    residual_hbm,
    normed_hbm,
    inverse_ref,
    ctx_hbm,
    vec,
    grad_one_ref,
    grad_ctx_ref,
    sums_ref,
    keep,
    send,
    keep_out,
    send_out,
    out_w,
    up_w,
    down_w,
    residual,
    normed,
    ctx,
    total,
    staged,
    bias_sums,
    sems,
):
    step = pl.program_id(0)
    me = me_ref[0]
    residual_in = pltpu.make_async_copy(residual_hbm, residual, sems.at[6])
    normed_in = pltpu.make_async_copy(normed_hbm, normed, sems.at[7])
    ctx_in = pltpu.make_async_copy(ctx_hbm, ctx, sems.at[8])

    @pl.when(step == 0)
    def _():
        start_pieces(me, near_down, far_down, 0, 4 * PIECE_ROWS, down_w, sems.at[5])
        for block in range(4):
            start_pieces(
                me,
                near_up,
                far_up,
                (1 + block) * PIECE_ROWS,
                PIECE_ROWS,
                up_w.at[block],
                sems.at[block],
            )
        start_pieces(me, near_up, far_up, 0, PIECE_ROWS, out_w, sems.at[4])
        residual_in.start()
        normed_in.start()
        ctx_in.start()
        wait_bytes(down_w, sems.at[5])

    for block in range(4):

        @pl.when(step == block)
        def _():
            wait_bytes(up_w.at[block], sems.at[block])

    at = pl.multiple_of(step * D, D)
    grads = []
    biases = jnp.zeros((1, D), jnp.float32)
    for first in range(0, ROWS, 256):
        part = slice(first, first + 256)
        active_grad = contract_cols(low_ref[part, :], down_w[pl.ds(at, D), :])
        grad = (active_grad * slope_ref[part, :].astype(jnp.float32)).astype(low_type)
        biases = biases + column_sum(grad)
        grads.append(grad)
        back = contract_cols(grad, up_w[step])

        @pl.when(step == 0)
        def _():
            total[part, :] = back

        @pl.when(step > 0)
        def _():
            total[part, :] += back

    grad = jnp.concatenate(grads, axis=0)
    for first in range(0, D, 256):
        staged[step, first : first + 256, :] = contract_rows(
            hidden_ref[:, first : first + 256], grad
        ).astype(low_type)
    bias_sums[step] = biases
    for block in range(4):

        @pl.when(step == block)
        def _():
            start_owners(
                me,
                staged.at[block],
                PIECE_ROWS,
                keep,
                send,
                block * PIECE_ROWS,
                sems.at[9 + block],
            )

    @pl.when(step == 3)
    def _():
        residual_in.wait()
        normed_in.wait()
        ctx_in.wait()
        wait_bytes(out_w, sems.at[4])
        gains = jnp.zeros((1, D), jnp.float32)
        shifts = jnp.zeros((1, D), jnp.float32)
        out_biases = jnp.zeros((1, D), jnp.float32)
        lows = []
        for first in range(0, ROWS, 256):
            part = slice(first, first + 256)
            upstream = residual[part, :] + total[part, :]
            n = normed[part, :]
            gains = gains + column_sum(upstream * n)
            shifts = shifts + column_sum(upstream)
            grad_one = norm_back(upstream, n, inverse_ref[part, :], vec[3:4, :])
            grad_one_ref[part, :] = grad_one
            rounded = grad_one.astype(low_type)
            out_biases = out_biases + column_sum(rounded)
            grad_ctx_ref[part, :] = contract_cols(rounded, out_w[...]).astype(low_type)
            lows.append(rounded)
        sums_ref[...] = jnp.concatenate(
            [bias_sums[block] for block in range(4)]
            + [out_biases, gains, shifts, jnp.zeros((1, D), jnp.float32)]
        )
        rounded = jnp.concatenate(lows, axis=0)
        for first in range(0, D, 256):
            staged[4, first : first + 256, :] = contract_rows(
                ctx[:, first : first + 256], rounded
            ).astype(low_type)
        start_owners(me, staged.at[4], PIECE_ROWS, keep_out, send_out, 0, sems.at[13])
        for block in range(5):
            wait_bytes(staged.at[block], sems.at[9 + block])


def up_back(
    me, near_up, far_up, near_down, far_down, low, slope, hidden, residual, normed, inverse, ctx, vec
):
    half = jax.ShapeDtypeStruct((8, 4 * PIECE_ROWS, D), low_type)
    half_out = jax.ShapeDtypeStruct((8, PIECE_ROWS, D), low_type)
    return pl.pallas_call(
        up_back_kernel,
        grid=(4,),
        in_specs=[scalar_space]
        + [any_space] * 4
        + [
            vmem_space,
            pl.BlockSpec((ROWS, D), lambda s: (0, s)),
            vmem_space,
            any_space,
            any_space,
            vmem_space,
            any_space,
            vmem_space,
        ],
        out_specs=[vmem_space] * 3 + [any_space] * 4,
        out_shape=[
            jax.ShapeDtypeStruct((ROWS, D), jnp.float32),
            jax.ShapeDtypeStruct((ROWS, D), low_type),
            jax.ShapeDtypeStruct((8, D), jnp.float32),
            half,
            half,
            half_out,
            half_out,
        ],
        scratch_shapes=[
            pltpu.VMEM((D, D), low_type),
            pltpu.VMEM((4, D, D), low_type),
            pltpu.VMEM((FF, D), low_type),
            pltpu.VMEM((ROWS, D), jnp.float32),
            pltpu.VMEM((ROWS, D), jnp.float32),
            pltpu.VMEM((ROWS, D), low_type),
            pltpu.VMEM((ROWS, D), jnp.float32),
            pltpu.VMEM((5, D, D), low_type),
            pltpu.VMEM((4, 1, D), jnp.float32),
            pltpu.SemaphoreType.DMA((14,)),
        ],
        compiler_params=params(56),
        cost_estimate=cost(2 * ROWS * D * (3 * FF + 2 * D), 40e6),
        name="up_back",
    )(
        me,
        near_up,
        far_up,
        near_down,
        far_down,
        low,
        slope,
        hidden,
        residual,
        normed,
        inverse,
        ctx,
        vec,
    )


def attention_back_kernel(
    group,
    me_ref,
    near,
    far,
    x_ref,
    seg_col,
    seg_row,
    mixed_ref,
    lse_ref,
    grad_ctx_ref,
    earlier_hbm,
    input_hbm,
    sums_ref,
    keep,
    send,
    w,
    total,
    weight_grad,
    staged,
    sems,
):
    mb = pl.program_id(0)
    me = me_ref[0]
    earlier_in = pltpu.make_async_copy(earlier_hbm, total, sems.at[1])

    @pl.when(mb == 0)
    def _():
        start_pieces(me, near, far, group * PIECE_ROWS, PIECE_ROWS, w, sems.at[0])
        earlier_in.start()

    mask = jnp.where(seg_col[...] == seg_row[...].reshape(1, L), 0.0, masked_score)
    mixed = mixed_ref[...].reshape(L, D)
    lse = lse_ref[...].reshape(L, HEADS)
    grad_q, grad_k, grad_v = [], [], []
    for head in range(HEADS):
        q = mixed[:, head * HD : (head + 1) * HD]
        k = mixed[:, QCOLS + head * HD : QCOLS + (head + 1) * HD]
        v = mixed[:, 2 * QCOLS + head * HD : 2 * QCOLS + (head + 1) * HD]
        grad_o = grad_ctx_ref[:, head * HD : (head + 1) * HD]
        dq, dk, dv = [], None, None
        for first in range(0, L, 256):
            part = slice(first, first + 256)
            scores = contract_cols(q[part], k) * (attention_scale * log2e) + mask[part]
            probs = jnp.exp2(scores - lse[part, head : head + 1])
            grad_probs = contract_cols(grad_o[part], v)
            inner = jnp.sum(probs * grad_probs, axis=-1, keepdims=True)
            grad_scores = (probs * (grad_probs - inner)).astype(low_type)
            dv_part = contract_rows(probs.astype(low_type), grad_o[part])
            dk_part = contract_rows(grad_scores, q[part])
            dq.append(rows_dot(grad_scores, k) * attention_scale)
            dk = dk_part if dk is None else dk + dk_part
            dv = dv_part if dv is None else dv + dv_part
        grad_q.append(jnp.concatenate(dq, axis=0))
        grad_k.append(dk * attention_scale)
        grad_v.append(dv)
    grad_mixed = jnp.concatenate(grad_q + grad_k + grad_v, axis=1).astype(low_type)

    @pl.when(mb == 0)
    def _():
        wait_bytes(w, sems.at[0])
        earlier_in.wait()

    rows = pl.ds(pl.multiple_of(mb * L, L), L)
    total[rows, :] += contract_cols(grad_mixed, w[...])
    bias = column_sum(grad_mixed)
    terms = contract_rows(x_ref[...], grad_mixed)

    @pl.when(mb == 0)
    def _():
        weight_grad[...] = terms
        sums_ref[0:1, :] = bias

    @pl.when(mb == 1)
    def _():
        out = pltpu.make_async_copy(total, input_hbm, sems.at[1])
        out.start()
        sums_ref[0:1, :] += bias
        staged[...] = (weight_grad[...] + terms).astype(low_type)
        start_owners(me, staged, PIECE_ROWS, keep, send, 0, sems.at[2])
        wait_bytes(staged, sems.at[2])
        out.wait()


def attention_back(
    me, near, far, x_low, seg_col, seg_row, mixed, lse, grad_ctx, earlier, group
):
    half = jax.ShapeDtypeStruct((8, PIECE_ROWS, D), low_type)
    return pl.pallas_call(
        partial(attention_back_kernel, group),
        grid=(MB,),
        in_specs=[
            scalar_space,
            any_space,
            any_space,
            pl.BlockSpec((L, D), lambda m: (m, 0)),
            pl.BlockSpec((L, 1), lambda m: (m, 0)),
            pl.BlockSpec((1, 1, L), lambda m: (m, 0, 0)),
            pl.BlockSpec((1, L, D), lambda m: (group, m, 0)),
            pl.BlockSpec((1, L, HEADS), lambda m: (group * MB + m, 0, 0)),
            pl.BlockSpec((L, QCOLS), lambda m: (m, group)),
            any_space,
        ],
        out_specs=[any_space, vmem_space, any_space, any_space],
        out_shape=[
            jax.ShapeDtypeStruct((ROWS, D), jnp.float32),
            jax.ShapeDtypeStruct((8, D), jnp.float32),
            half,
            half,
        ],
        scratch_shapes=[
            pltpu.VMEM((D, D), low_type),
            pltpu.VMEM((ROWS, D), jnp.float32),
            pltpu.VMEM((D, D), jnp.float32),
            pltpu.VMEM((D, D), low_type),
            pltpu.SemaphoreType.DMA((3,)),
        ],
        compiler_params=params(40),
        cost_estimate=cost(
            4 * ROWS * D * D + 20 * MB * HEADS * L * L * HD, 12e6, MB * HEADS * L * L
        ),
        name=f"attention_back_{group}",
    )(me, near, far, x_low, seg_col, seg_row, mixed, lse, grad_ctx, earlier)


def by_heads(matrix):
    shaped = matrix.reshape(matrix.shape[0], 3, HG, D // HG)
    return jnp.transpose(shaped, (2, 0, 1, 3)).reshape(HG, matrix.shape[0], D)


def from_heads(blocks):
    rows = blocks.shape[1]
    shaped = blocks.reshape(HG, rows, 3, D // HG)
    return jnp.transpose(shaped, (1, 2, 0, 3)).reshape(rows, 3 * D)


def by_columns(matrix):
    return jnp.transpose(matrix.reshape(matrix.shape[0], 4, D), (1, 0, 2))


def from_columns(blocks):
    return jnp.transpose(blocks, (1, 0, 2)).reshape(blocks.shape[1], 4 * D)


def adam_update(master, grad_share, first, second, rate, factor):
    clipped = grad_share * factor
    first_new = beta_first * first + (1.0 - beta_first) * clipped
    second_new = beta_second * second + (1.0 - beta_second) * clipped * clipped
    first_hat = first_new / (1.0 - beta_first**STEP)
    second_hat = second_new / (1.0 - beta_second**STEP)
    master_new = master - rate * (
        first_hat / (jnp.sqrt(second_hat) + adam_eps) + weight_decay * master
    )
    return (master_new[None], first_new[None], second_new[None])


def halves(matrix_rows):
    k = matrix_rows.shape[0]
    shaped = matrix_rows.reshape(k, 2, 2, 2, 2, -1, D)
    pieces = jnp.transpose(shaped, (4, 3, 2, 1, 0, 5, 6)).reshape(PIECES, -1, D)
    return (pieces[:8], pieces[8:])


def whole_rows(keep, send, k):
    shaped = jnp.concatenate([keep, send]).reshape(2, 2, 2, 2, k, -1, D)
    return jnp.transpose(shaped, (4, 3, 2, 1, 0, 5, 6)).reshape(k, -1, D)


def beside(sends, *work):
    received = [swapped(value, mask) for value, mask in sends]
    done = lax.optimization_barrier((received, work))
    return (done[0], *done[1])


def joined(pieces, received):
    return jnp.concatenate([pieces, received])


def parted(keep, received):
    half = keep.shape[0] // 2
    return (
        added(keep[:half], received[:half]).astype(low_type),
        added(keep[half:], received[half:]).astype(low_type),
    )


def body(
    tokens,
    segments,
    positives,
    token_grad,
    mix_weight,
    out_weight,
    up_weight,
    down_weight,
    vectors,
    first_mix,
    first_out,
    first_up,
    first_down,
    first_vectors,
    second_mix,
    second_out,
    second_up,
    second_down,
    second_vectors,
):
    owners = lax.axis_size("dp")
    fast = owners == PIECES
    index = lax.axis_index("dp")
    flag = lax.axis_index("tower").astype(jnp.int32).reshape(1)
    masters = (mix_weight[0], out_weight[0], up_weight[0], down_weight[0], vectors[0])
    low_mix, low_out, low_up, low_down, low_vec = (m.astype(low_type) for m in masters)
    share = low_vec.shape[1]
    queries_all = owners * SEGS

    if fast:
        me = index.astype(jnp.int32).reshape(1)
        extra = jnp.zeros((16, D), low_type)
        extra = extra.at[12:14, :SEGS].set(positives.astype(low_type))
        extra = lax.dynamic_update_slice(extra, low_vec, (0, index * share))
        pack_mix = jnp.concatenate([by_heads(low_mix).reshape(-1, D), extra])
        pack_up = jnp.concatenate([low_out, by_columns(low_up).reshape(-1, D)])
        mix, up, down = pack_mix[None], pack_up[None], low_down[None]
        ((got_mix,),) = beside([(mix, 8)])
        mix = joined(mix, got_mix)
        ((got_mix, got_up),) = beside([(mix, 4), (up, 8)])
        mix, up = joined(mix, got_mix), joined(up, got_up)
        ((got_mix, got_up, got_down),) = beside([(mix, 2), (up, 4), (down, 8)])
        mix_near, up, down = joined(mix, got_mix), joined(up, got_up), joined(down, got_down)
        mix_far = swapped(mix_near, 1)
        extras = jnp.concatenate([mix_near[:, 144:], mix_far[:, 144:]])
        vec_f = jnp.sum(extras[:, :12].astype(jnp.float32), axis=0)
        cls_positives = jnp.transpose(extras[:, 12:14, :SEGS].astype(jnp.int32), (1, 0, 2))
        cls_positives = cls_positives.reshape(MB, queries_all, 1)
        relative = relative_of(jnp.arange(PIECES, dtype=jnp.int32))
        cls_ids = ((relative ^ index)[:, None] * SEGS + jnp.arange(SEGS)[None, :]).reshape(1, -1)
    else:
        me = jnp.zeros((1,), jnp.int32)
        mix_near, mix_far = halves(by_heads(lax.all_gather(low_mix, "dp", axis=0, tiled=True)))
        out_near, out_far = halves(lax.all_gather(low_out, "dp", axis=0, tiled=True)[None])
        up_near, up_far = halves(by_columns(lax.all_gather(low_up, "dp", axis=0, tiled=True)))
        up_near = jnp.concatenate([out_near, up_near], axis=1)
        up_far = jnp.concatenate([out_far, up_far], axis=1)
        down_near, down_far = halves(lax.all_gather(low_down, "dp", axis=0, tiled=True)[None])
        vec_f = lax.all_gather(low_vec, "dp", axis=1, tiled=True).astype(jnp.float32)
        cls_positives = lax.all_gather(positives, "dp", axis=1, tiled=True)
        cls_positives = jnp.roll(cls_positives, -index * SEGS, axis=1)[:, :, None]
        cls_ids = jnp.roll(jnp.arange(queries_all, dtype=jnp.int32), -index * SEGS)[None]

    x_low = tokens[0].reshape(ROWS, D)
    seg_rows = segments[0].reshape(MB, L)
    seg_col, seg_row = seg_rows.reshape(ROWS, 1), seg_rows.reshape(MB, 1, L)
    before = jnp.concatenate([jnp.full((MB, 1), -1, jnp.int32), seg_rows[:, :-1]], axis=1)
    numbers = jnp.where(seg_rows != before, seg_rows, -1)
    numbers = jnp.where(numbers >= 0, numbers + SEGS * jnp.arange(MB)[:, None], -1).reshape(1, ROWS)
    table = (jnp.arange(MB * SEGS)[:, None] == numbers).astype(low_type)
    mixed_bias = jnp.concatenate([vec_f[0], jnp.zeros_like(vec_f[0]), vec_f[1]])
    mixed_bias = jnp.transpose(mixed_bias.reshape(3, HG, QCOLS), (1, 0, 2)).reshape(HG, 1, D)
    mixed, context, lse = attention_forward(
        me, mix_near, mix_far, x_low, seg_col, seg_row, mixed_bias
    )
    if fast:
        (got_up, got_down), mixed, context, lse = beside(
            [(up, 2), (down, 4)], mixed, context, lse
        )
        up_near, down = joined(up, got_up), joined(down, got_down)
        up_far = swapped(up_near, 1)
    normed_one, inverse_one, hidden, active, slope = up_forward(
        me, up_near, up_far, context, x_low, vec_f
    )
    if fast:
        (got_down,), normed_one, hidden, active, slope = beside(
            [(down, 2)], normed_one, hidden, active, slope
        )
        down_near = joined(down, got_down)
        down_far = swapped(down_near, 1)
    normed_two, inverse_two, output, cls_low = down_forward(
        me, down_near, down_far, active, normed_one, vec_f, table
    )

    both = jnp.concatenate([cls_low, tower_swapped(cls_low)])
    if fast:
        everyone = gather_pieces(both)
    else:
        everyone = jnp.roll(lax.all_gather(both, "dp", axis=0, tiled=False), -index, axis=0)
    everyone = jnp.transpose(everyone.reshape(owners, 2, MB, SEGS, D), (1, 2, 0, 3, 4))
    everyone = everyone.reshape(2, MB, queries_all, D)
    grad_cls = contrast_back(flag, everyone, cls_positives, cls_ids)

    residual, grad_ffn, sums_two, keep_down, send_down = down_back(
        me,
        token_grad[0].reshape(ROWS, D),
        grad_cls,
        jnp.concatenate([table] * 3),
        normed_two,
        inverse_two,
        vec_f,
        active,
    )
    if fast:
        (got_down,), residual, grad_ffn = beside([(send_down, 1)], residual, grad_ffn)
        keep_down, send_down = parted(keep_down, got_down)
    (grad_one, grad_ctx, sums_one, keep_up, send_up, keep_out, send_out) = up_back(
        me,
        up_near,
        up_far,
        down_near,
        down_far,
        grad_ffn,
        slope,
        hidden,
        residual,
        normed_one,
        inverse_one,
        context,
        vec_f,
    )
    if fast:
        (got_down,), grad_one, grad_ctx, send_up, send_out = beside(
            [(send_down, 2)], grad_one, grad_ctx, send_up, send_out
        )
        keep_down, send_down = parted(keep_down, got_down)
    back = partial(
        attention_back, me, mix_near, mix_far, x_low, seg_col, seg_row, mixed, lse, grad_ctx
    )
    grad_first, sums_a, keep_a, send_a = back(grad_one, 0)
    if fast:
        (got_down, got_up), grad_first, send_a = beside(
            [(send_down, 4), (send_up, 1)], grad_first, send_a
        )
        keep_down, send_down = parted(keep_down, got_down)
        keep_up, send_up = parted(keep_up, got_up)
        keep_a = jnp.concatenate([keep_out, keep_a], axis=1)
        send_a = jnp.concatenate([send_out, send_a], axis=1)
    grad_second, sums_b, keep_b, send_b = back(grad_first, 1)
    if fast:
        (got_down, got_up, got_a), grad_second, send_b = beside(
            [(send_down, 8), (send_up, 2), (send_a, 1)], grad_second, send_b
        )
        share_down = added(keep_down[0], got_down[0])
        keep_up, send_up = parted(keep_up, got_up)
        keep_a, send_a = parted(keep_a, got_a)
    input_grad, sums_c, keep_c, send_c = back(grad_second, 2)
    bias_mixed = jnp.concatenate([sums_a[:1], sums_b[:1], sums_c[:1]]).reshape(HG, 3, QCOLS)
    grad_vec = jnp.concatenate(
        [
            bias_mixed[:, 0].reshape(1, D),
            bias_mixed[:, 2].reshape(1, D),
            sums_one[4:7],
            sums_one[0:4],
            sums_two[0:3],
        ],
        axis=0,
    )
    if fast:
        vec_rows = jnp.broadcast_to(
            jnp.pad(grad_vec, ((0, 4), (0, 0))).astype(low_type)[None], (8, 16, D)
        )
        (got_up, got_a, got_b), input_grad, send_c = beside(
            [(send_up, 4), (send_a, 2), (send_b, 1)], input_grad, send_c
        )
        keep_up, send_up = parted(keep_up, got_up)
        keep_a, send_a = parted(keep_a, got_a)
        keep_b, send_b = parted(keep_b, got_b)
        keep_c = jnp.concatenate([keep_c, vec_rows], axis=1)
        send_c = jnp.concatenate([send_c, vec_rows], axis=1)
        ((got_up, got_a, got_b, got_c),) = beside(
            [(send_up, 8), (send_a, 4), (send_b, 2), (send_c, 1)]
        )
        share_up = added(keep_up[0], got_up[0])
        keep_a, send_a = parted(keep_a, got_a)
        keep_b, send_b = parted(keep_b, got_b)
        keep_c, send_c = parted(keep_c, got_c)
        ((got_a, got_b, got_c),) = beside([(send_a, 8), (send_b, 4), (send_c, 2)])
        share_a = added(keep_a[0], got_a[0])
        keep_b, send_b = parted(keep_b, got_b)
        keep_c, send_c = parted(keep_c, got_c)
        ((got_b, got_c),) = beside([(send_b, 8), (send_c, 4)])
        share_b = added(keep_b[0], got_b[0])
        keep_c, send_c = parted(keep_c, got_c)
        share_c = added(keep_c[0], swapped(send_c, 8)[0])
        share_out = share_a[:48]
        share_mix = from_heads(jnp.stack([share_a[48:], share_b, share_c[:48]]))
        share_vec = lax.dynamic_slice(share_c[48:60], (0, index * share), (12, share))
        share_up = from_columns(share_up.reshape(4, PIECE_ROWS, D))
    else:

        def scattered(matrix):
            return lax.psum_scatter(
                matrix.astype(jnp.float32), "dp", scatter_dimension=0, tiled=True
            )

        mix_blocks = jnp.concatenate(
            [whole_rows(*half, 1) for half in ((keep_a, send_a), (keep_b, send_b), (keep_c, send_c))]
        )
        share_mix = scattered(from_heads(mix_blocks))
        share_out = scattered(whole_rows(keep_out, send_out, 1)[0])
        share_up = scattered(from_columns(whole_rows(keep_up, send_up, 4)))
        share_down = scattered(whole_rows(keep_down, send_down, 1)[0])
        share_vec = lax.psum_scatter(grad_vec, "dp", scatter_dimension=1, tiled=True)

    shares = (share_mix, share_out, share_up, share_down, share_vec)
    local_square = sum(jnp.sum(s * s) for s in shares)
    if fast:
        grad_square = jnp.broadcast_to(local_square, (8, 128))
        for mask in (1, 2, 4, 8):
            grad_square = grad_square + swapped(grad_square, mask)
        grad_square = grad_square + tower_swapped(grad_square)
        grad_square = grad_square[0, 0]
    else:
        grad_square = lax.psum(local_square, ("tower", "dp"))
    factor = jnp.minimum(1.0, clip_norm / (jnp.sqrt(grad_square) + 1e-06))
    firsts = (first_mix[0], first_out[0], first_up[0], first_down[0], first_vectors[0])
    seconds = (second_mix[0], second_out[0], second_up[0], second_down[0], second_vectors[0])
    rates = (matrix_rate, matrix_rate, matrix_rate, matrix_rate, vector_rate)
    results = [
        adam_update(masters[i], shares[i], firsts[i], seconds[i], rates[i], factor)
        for i in range(5)
    ]
    return (
        output.reshape(1, MB, 1, L, D),
        input_grad.reshape(1, MB, 1, L, D),
        *(r[0] for r in results),
        *(r[1] for r in results),
        *(r[2] for r in results),
        grad_square,
    )


def solution(mesh):
    rows = P("tower", None, "dp", None, None)
    shards = (P("tower", "dp", None),) * 4 + (P("tower", None, "dp"),)
    in_specs = (rows, P("tower", None, "dp", None), P(None, "dp"), rows) + shards * 3
    out_specs = (rows, rows) + shards * 3 + (P(),)
    return jax.shard_map(body, mesh=mesh, in_specs=in_specs, out_specs=out_specs, check_vma=False)
```

time: 740 us -> 402 us (0.54)
  matrix products: 196 us -> 0 us
  Pallas kernels: 0 us -> 170 us
  local copies, waits for them, and re-layouts: 163 us -> 19.7 us
  waiting for transfers between devices: 216 us -> 117 us
  other arithmetic: 98.7 us -> 35.3 us
    dot_general x21 -> x0, matrix products: 194 us -> none  [the longest x4 54.4 us: plain_dot(): return jnp.dot(first_op, second_op, preferred_element_type=jnp.float32)]
    pallas_call x0 -> x9, Pallas kernels: none -> 170 us  [the longest x3 52.9 us: attention_back(): pl.pallas_call(partial(attention_back_kernel, group), grid=(MB,), in_spec...]
    ppermute x39 -> x40, waiting for transfers between devices: 214 us -> 113 us  [swapped(): return lax.ppermute(value, 'dp', pairs)]
    gather x7 -> x0, local copies, waits for them, and re-layouts: 31.3 us -> none  [the longest x3 16.7 us: body(): jnp.take(g, places, axis=0)]
    another operation x3 -> x6, local copies, waits for them, and re-layouts: 23.3 us -> 0.53 us  [the longest x4 0.29 us: body(): share_mix = from_heads(jnp.stack([share_a[48:], share_b, share_c[:48]]))]
    convert_element_type x8 -> x16, other arithmetic: 29.9 us -> 8.39 us  [the longest x7 4.51 us: parted(): added(keep[:half], received[:half]).astype(low_type)]
    reduce_sum x9 -> x1, other arithmetic: 21.1 us -> 0.07 us  [body(): vec_f = jnp.sum(extras[:, :12].astype(jnp.float32), axis=0)]
    reshape x7 -> x3, local copies, waits for them, and re-layouts: 20.5 us -> 0.12 us  [the longest x2 0.09 us: body(): cls_positives = cls_positives.reshape(MB, queries_all, 1)]
  transfers between devices with their start and end apart: 41 -> 42, of which waited for: 21 -> 27; matrix products, arithmetic and copies ran while one was open for 27% -> 4% of each run, Pallas kernels for 0% -> 36%
where the time goes in v2:
time: 402 us; the launch traced here: 396 us
  Pallas kernels  170 us (42%)
  waiting for transfers between devices  117 us (29%)
  starting transfers between devices  48.1 us (12%)
  other arithmetic  35.3 us (9%)
  local copies, waits for them, and re-layouts  19.7 us (5%)
  between operations  6.11 us (2%)
    ppermute x40, waiting for transfers between devices, swapped(): return lax.ppermute(value, 'dp', pairs)  113 us
    pallas_call x3, Pallas kernels, attention_back(): pl.pallas_call(partial(attention_back_kernel, group), grid=(MB,), in_spec...  52.9 us
    ppermute x40, starting transfers between devices, swapped(): return lax.ppermute(value, 'dp', pairs)  45.2 us
    pallas_call x1, Pallas kernels, up_back(): pl.pallas_call(up_back_kernel, grid=(4,), in_specs=[scalar_space] + [any_...  35.5 us
    pallas_call x1, Pallas kernels, attention_forward(): pl.pallas_call(attention_kernel, grid=(HG, MB), in_specs=[scalar_space, a...  29.6 us
    pallas_call x1, Pallas kernels, up_forward(): pl.pallas_call(up_kernel, grid=(4,), in_specs=[scalar_space, any_space, a...  23.8 us
    pallas_call x1, Pallas kernels, down_back(): pl.pallas_call(down_back_kernel, grid=(4,), in_specs=[scalar_space] + [vm...  15 us
    unnamed x139, local copies, waits for them, and re-layouts  13.9 us
  transfers between devices with their start and end apart: 42, of which 27 were waited for; matrix products, arithmetic and copies ran while one was open for 4% of the time, Pallas kernels for 36%

profile of v2, /device:TPU:0, one launch (start us, length us, event | category | flops | bytes accessed | tf_op | source)
XLA Modules:
  0.0 396.0 jit_solution(6271215671287096330)
XLA Ops:
  3.8 4.1 %collective-permute-start = (bf16[1,160,768]{2,1,0:T(8,128)(2,1)S(1)}, bf16[1,160,768]{2,1,0:T(8,128)(2,1)S(1)}, u32[]{:S(2)}, u32[]{:S(2)}) collective-permute-start(bf16[1,160,768]{2,1,0:T(8,128)(2,1)S(1)} %maximum_bitcast_fusion.1), channel_id=1, source_target_pairs={{0,8},{1,9},{2,10},{3,11},{4,12},{5,13},{6,14},{7,15},{8,0},{9,1},... | collective-permute-start | bytes 737288 | tf_op jit(solution)/shard_map/ppermute | solution.py:41
  7.9 11.5 %collective-permute-done = bf16[1,160,768]{2,1,0:T(8,128)(2,1)S(1)} collective-permute-done((bf16[1,160,768]{2,1,0:T(8,128)(2,1)S(1)}, bf16[1,160,768]{2,1,0:T(8,128)(2,1)S(1)}, u32[]{:S(2)}, u32[]{:S(2)}) %collective-permute-start) | collective-permute-done | bytes 245792 | tf_op jit(solution)/shard_map/ppermute | solution.py:41
  20.6 3.4 collective-permute-start.2
  24.1 14.7 %collective-permute-done.2 = bf16[1,240,768]{2,1,0:T(8,128)(2,1)S(1)} collective-permute-done((bf16[1,240,768]{2,1,0:T(8,128)(2,1)S(1)}, bf16[1,240,768]{2,1,0:T(8,128)(2,1)S(1)}, u32[]{:S(2)}, u32[]{:S(2)}) %collective-permute-start.2) | collective-permute-done | bytes 368672 | tf_op jit(solution)/shard_map/ppermute | solution.py:41
  41.4 3.4 collective-permute-start.4
  46.6 19.6 %collective-permute-done.5 = bf16[1,192,768]{2,1,0:T(8,128)(2,1)S(1)} collective-permute-done((bf16[1,192,768]{2,1,0:T(8,128)(2,1)S(1)}, bf16[1,192,768]{2,1,0:T(8,128)(2,1)S(1)}, u32[]{:S(2)}, u32[]{:S(2)}) %collective-permute-start.5) | collective-permute-done | bytes 294944 | tf_op jit(solution)/shard_map/ppermute | solution.py:41
  76.1 29.6 %mixed_attention.1 = (bf16[3,1024,768]{2,1,0:T(8,128)(2,1)S(1)}, bf16[1024,768]{1,0:T(8,128)(2,1)S(1)}, f32[6,512,4]{2,1,0:T(8,128)S(1)}) custom-call(s32[1]{0:T(128)} %bitcast.me_ref, bf16[8,160,768]{2,1,0:T(8,128)(2,1)S(1)} %pad_maximum_fusion.2.near, bf16[8,160,768]{2,1,0:T(8,128)(2,1)} %collective-permute-done.8.far, bf16[1024,768]{1,0:T(8,128)(2,1)S(1)} %bitcast.151, ...), custom_call_target="tpu_custom_call" | custom-call | flops 6845104128 | bytes 12000000 | tf_op jit(solution)/shard_map/mixed_attention/pallas_call | solution.py:199
  107.8 2.7 pad_maximum_fusion.near.near_up
  117.6 23.8 %out_up.1 = (f32[1024,768]{1,0:T(8,128)}, f32[1024,1]{1,0:T(8,128)S(1)}, bf16[1024,768]{1,0:T(8,128)(2,1)S(1)}, bf16[1024,3072]{1,0:T(8,128)(2,1)}, bf16[1024,3072]{1,0:T(8,128)(2,1)}) custom-call(s32[1]{0:T(128)} %bitcast.me_ref, bf16[8,240,768]{2,1,0:T(8,128)(2,1)S(1)} %pad_maximum_fusion.near.near_up, bf16[8,240,768]{2,1,0:T(8,128)(2,1)} %copy-done.61, ...), custom_call_target="tpu_custom_call" | custom-call | flops 6039797760 | bytes 24000000 | tf_op jit(solution)/shard_map/out_up/pallas_call | solution.py:308
  143.7 4.2 %collective-permute-done.11.far.far_down = bf16[8,192,768]{2,1,0:T(8,128)(2,1)S(1)} collective-permute-done((bf16[8,192,768]{2,1,0:T(8,128)(2,1)S(1)}, bf16[8,192,768]{2,1,0:T(8,128)(2,1)S(1)}, u32[]{:S(2)}, u32[]{:S(2)}) %collective-permute-start.11) | collective-permute-done | bytes 2359328 | tf_op jit(solution)/shard_map/ppermute | solution.py:41
  147.9 11.8 %down.1 = (f32[1024,768]{1,0:T(8,128)S(1)}, f32[1024,1]{1,0:T(8,128)S(1)}, bf16[1024,768]{1,0:T(8,128)(2,1)}, bf16[16,768]{1,0:T(8,128)(2,1)S(1)}) custom-call(s32[1]{0:T(128)} %bitcast.me_ref, bf16[8,192,768]{2,1,0:T(8,128)(2,1)S(1)} %pad_maximum_fusion.1.near.near_down, bf16[8,192,768]{2,1,0:T(8,128)(2,1)S(1)} %collective-permute-done.11.far.far_down, ...), custom_call_target="tpu_custom_call" | custom-call | flops 4831838208 | bytes 19000000 | tf_op jit(solution)/shard_map/down/pallas_call | solution.py:380
  167.2 3.5 collective-permute-done.13
  171.2 4.2 %collective-permute-done.14 = bf16[2,32,768]{2,1,0:T(8,128)(2,1)S(1)} collective-permute-done((bf16[2,32,768]{2,1,0:T(8,128)(2,1)S(1)}, bf16[2,32,768]{2,1,0:T(8,128)(2,1)S(1)}, u32[]{:S(2)}, u32[]{:S(2)}) %collective-permute-start.14) | collective-permute-done | bytes 98336 | tf_op jit(solution)/shard_map/ppermute | solution.py:41
  176.9 4.4 %collective-permute-done.15 = bf16[4,32,768]{2,1,0:T(8,128)(2,1)S(1)} collective-permute-done((bf16[4,32,768]{2,1,0:T(8,128)(2,1)S(1)}, bf16[4,32,768]{2,1,0:T(8,128)(2,1)S(1)}, u32[]{:S(2)}, u32[]{:S(2)}) %collective-permute-start.15) | collective-permute-done | bytes 196640 | tf_op jit(solution)/shard_map/ppermute | solution.py:41
  184.3 15.0 %down_back.1 = (f32[1024,768]{1,0:T(8,128)}, bf16[1024,768]{1,0:T(8,128)(2,1)S(1)}, f32[8,768]{1,0:T(8,128)S(1)}, bf16[8,192,768]{2,1,0:T(8,128)(2,1)S(1)}, bf16[8,192,768]{2,1,0:T(8,128)(2,1)}) custom-call(s32[1]{0:T(128)} %bitcast.me_ref, f32[1024,768]{1,0:T(8,128)} %bitcast.175, f32[16,768]{1,0:T(8,128)S(1)} %contrast.1.grad_cls, ...), custom_call_target="tpu_custom_call" | custom-call | flops 4831838208 | bytes 25000000 | tf_op jit(solution)/shard_map/down_back/pallas_call | solution.py:490
  199.5 4.6 %collective-permute-done.17 = bf16[8,192,768]{2,1,0:T(8,128)(2,1)S(1)} collective-permute-done((bf16[8,192,768]{2,1,0:T(8,128)(2,1)}, bf16[8,192,768]{2,1,0:T(8,128)(2,1)S(1)}, u32[]{:S(2)}, u32[]{:S(2)}) %collective-permute-start.17) | collective-permute-done | bytes 2359328 | tf_op jit(solution)/shard_map/ppermute | solution.py:41
  206.0 35.5 %up_back.1 = (f32[1024,768]{1,0:T(8,128)}, bf16[1024,768]{1,0:T(8,128)(2,1)}, f32[8,768]{1,0:T(8,128)}, bf16[8,192,768]{2,1,0:T(8,128)(2,1)}, bf16[8,192,768]{2,...) custom-call(s32[1]{0:T(128)} %bitcast.me_ref, bf16[8,240,768]{2,1,0:T(8,128)(2,1)} %copy-done, ...), custom_call_target="tpu_custom_call" | custom-call | flops 16911433728 | bytes 40000000 | tf_op jit(solution)/shard_map/up_back/pallas_call | solution.py:658
  245.0 17.7 %attention_back_0.1 = (f32[1024,768]{1,0:T(8,128)S(1)}, f32[8,768]{1,0:T(8,128)S(1)}, bf16[8,48,768]{2,1,0:T(8,128)(2,1)S(1)}, bf16[8,48,768]{2,1,0:T(8,128)(2,1)S(1)}) custom-call(s32[1]{0:T(128)} %bitcast.me_ref, bf16[8,160,768]{2,1,0:T(8,128)(2,1)S(1)} %copy-done.2, bf16[8,160,768]{2,1,0:T(8,128)(2,1)} %collective-permute-done.8.far, ...), custom_call_target="tpu_custom_call" | custom-call | flops 5100273664 | bytes 12000000 | tf_op jit(solution)/shard_map/attention_back_0/pallas_call | solution.py:803
  267.6 17.7 %attention_back_1.1 = (f32[1024,768]{1,0:T(8,128)S(1)}, f32[8,768]{1,0:T(8,128)S(1)}, bf16[8,48,768]{2,1,0:T(8,128)(2,1)S(1)}, bf16[8,48,768]{2,1,0:T(8,128)(2,1)S(1)}) custom-call(s32[1]{0:T(128)} %bitcast.me_ref, bf16[8,160,768]{2,1,0:T(8,128)(2,1)S(1)} %copy-done.2, bf16[8,160,768]{2,1,0:T(8,128)(2,1)} %collective-permute-done.8.far, ...), custom_call_target="tpu_custom_call" | custom-call | flops 5100273664 | bytes 12000000 | tf_op jit(solution)/shard_map/attention_back_1/pallas_call | solution.py:803
  285.4 7.4 %collective-permute-done.22 = bf16[4,192,768]{2,1,0:T(8,128)(2,1)S(1)} collective-permute-done((bf16[4,192,768]{2,1,0:T(8,128)(2,1)S(1)}, bf16[4,192,768]{2,1,0:T(8,128)(2,1)S(1)}, u32[]{:S(2)}, u32[]{:S(2)}) %collective-permute-start.22) | collective-permute-done | bytes 1179680 | tf_op jit(solution)/shard_map/ppermute | solution.py:41
  296.3 17.5 %attention_back_2.1 = (f32[1024,768]{1,0:T(8,128)}, f32[8,768]{1,0:T(8,128)S(1)}, bf16[8,48,768]{2,1,0:T(8,128)(2,1)S(1)}, bf16[8,48,768]{2,1,0:T(8,128)(2,1)S(1)}) custom-call(s32[1]{0:T(128)} %bitcast.me_ref, bf16[8,160,768]{2,1,0:T(8,128)(2,1)S(1)} %copy-done.2, bf16[8,160,768]{2,1,0:T(8,128)(2,1)} %collective-permute-done.8.far, ...), custom_call_target="tpu_custom_call" | custom-call | flops 5100273664 | bytes 12000000 | tf_op jit(solution)/shard_map/attention_back_2/pallas_call | solution.py:803
  315.4 3.1 collective-permute-start.27
  323.9 8.8 %collective-permute-done.27 = bf16[1,192,768]{2,1,0:T(8,128)(2,1)S(1)} collective-permute-done((bf16[1,192,768]{2,1,0:T(8,128)(2,1)S(1)}, bf16[1,192,768]{2,1,0:T(8,128)(2,1)S(1)}, u32[]{:S(2)}, u32[]{:S(2)}) %collective-permute-start.27) | collective-permute-done | bytes 294944 | tf_op jit(solution)/shard_map/ppermute | solution.py:41
  332.6 2.3 collective-permute-done.28
  339.8 3.7 collective-permute-done.31
  349.6 3.8 collective-permute-done.34
  356.6 3.7 collective-permute-done.36
  367.8 2.4 collective-permute-done.38
  370.2 2.3 collective-permute-start.39
  376.0 2.6 collective-permute-done.40
  385.0 3.1 multiply_subtract_fusion
  391.7 2.5 multiply_subtract_fusion.2
  (311 shorter events, 95.1 us)
Async XLA Ops:
  3.8 15.6 %collective-permute-start = (bf16[1,160,768]{2,1,0:T(8,128)(2,1)S(1)}, bf16[1,160,768]{2,1,0:T(8,128)(2,1)S(1)}, u32[]{:S(2)}, u32[]{:S(2)}) collective-permute-start(bf16[1,160,768]{2,1,0:T(8,128)(2,1)S(1)} %maximum_bitcast_fusion.1), channel_id=1, source_target_pairs={{0,8},{1,9},{2,10},{3,11},{4,12},{5,13},{6,14},{7,15},{8,0},{9,1},... | collective-permute-start | bytes 737288 | tf_op jit(solution)/shard_map/ppermute | solution.py:41
  19.5 20.7 %collective-permute-start.1 = (bf16[2,160,768]{2,1,0:T(8,128)(2,1)S(1)}, bf16[2,160,768]{2,1,0:T(8,128)(2,1)S(1)}, u32[]{:S(2)}, u32[]{:S(2)}) collective-permute-start(bf16[2,160,768]{2,1,0:T(8,128)(2,1)S(1)} %pad_maximum_fusion.10), channel_id=1, source_target_pairs={{0,4},{1,5},{2,6},{3,7},{4,0},{5,1},{6,2},{7,3},{8,12},{9,13},{10,... | collective-permute-start | bytes 1474568 | tf_op jit(solution)/shard_map/ppermute | solution.py:41
  20.6 18.2 %collective-permute-start.2 = (bf16[1,240,768]{2,1,0:T(8,128)(2,1)S(1)}, bf16[1,240,768]{2,1,0:T(8,128)(2,1)S(1)}, u32[]{:S(2)}, u32[]{:S(2)}) collective-permute-start(bf16[1,240,768]{2,1,0:T(8,128)(2,1)S(1)} %maximum_bitcast_fusion), channel_id=1, source_target_pairs={{0,8},{1,9},{2,10},{3,11},{4,12},{5,13},{6,14},{7,15},{8,0},{9,1},... | collective-permute-start | bytes 1105928 | tf_op jit(solution)/shard_map/ppermute | solution.py:41
  40.3 26.7 %collective-permute-start.3 = (bf16[4,160,768]{2,1,0:T(8,128)(2,1)S(1)}, bf16[4,160,768]{2,1,0:T(8,128)(2,1)S(1)}, u32[]{:S(2)}, u32[]{:S(2)}) collective-permute-start(bf16[4,160,768]{2,1,0:T(8,128)(2,1)S(1)} %pad_maximum_fusion.7), channel_id=1, source_target_pairs={{0,2},{1,3},{2,0},{3,1},{4,6},{5,7},{6,4},{7,5},{8,10},{9,11},{10,... | collective-permute-start | bytes 2949128 | tf_op jit(solution)/shard_map/ppermute | solution.py:41
  41.4 25.6 %collective-permute-start.4 = (bf16[2,240,768]{2,1,0:T(8,128)(2,1)S(1)}, bf16[2,240,768]{2,1,0:T(8,128)(2,1)S(1)}, u32[]{:S(2)}, u32[]{:S(2)}) collective-permute-start(bf16[2,240,768]{2,1,0:T(8,128)(2,1)S(1)} %pad_maximum_fusion.8), channel_id=1, source_target_pairs={{0,4},{1,5},{2,6},{3,7},{4,0},{5,1},{6,2},{7,3},{8,12},{9,13},{10,... | collective-permute-start | bytes 2211848 | tf_op jit(solution)/shard_map/ppermute | solution.py:41
  44.9 21.4 %collective-permute-start.5 = (bf16[1,192,768]{2,1,0:T(8,128)(2,1)S(1)}, bf16[1,192,768]{2,1,0:T(8,128)(2,1)S(1)}, u32[]{:S(2)}, u32[]{:S(2)}) collective-permute-start(bf16[1,192,768]{2,1,0:T(8,128)(2,1)S(1)} %convert_element_type.355), channel_id=1, source_target_pairs={{0,8},{1,9},{2,10},{3,11},{4,12},{5,13},{6,14},{7,15},{8,0},{9,1},... | collective-permute-start | bytes 884744 | tf_op jit(solution)/shard_map/ppermute | solution.py:41
  68.5 4.9 %collective-permute-start.8 = (bf16[8,160,768]{2,1,0:T(8,128)(2,1)S(1)}, bf16[8,160,768]{2,1,0:T(8,128)(2,1)}, u32[]{:S(2)}, u32[]{:S(2)}) collective-permute-start(bf16[8,160,768]{2,1,0:T(8,128)(2,1)S(1)} %pad_maximum_fusion.2.near), channel_id=1, source_target_pairs={{0,1},{1,0},{2,3},{3,2},{4,5},{5,4},{6,7},{7,6},{8,9},{9,8},{10,11... | collective-permute-start | bytes 5898248 | tf_op jit(solution)/shard_map/ppermute | solution.py:41
  70.1 37.7 %collective-permute-start.6 = (bf16[4,240,768]{2,1,0:T(8,128)(2,1)}, bf16[4,240,768]{2,1,0:T(8,128)(2,1)}, u32[]{:S(2)}, u32[]{:S(2)}) collective-permute-start(bf16[4,240,768]{2,1,0:T(8,128)(2,1)} %pad_maximum_fusion.3), channel_id=1, source_target_pairs={{0,2},{1,3},{2,0},{3,1},{4,6},{5,7},{6,4},{7,5},{8,10},{9,11},{10,... | collective-permute-start | bytes 4423688 | tf_op jit(solution)/shard_map/ppermute | solution.py:41
  72.0 35.8 %collective-permute-start.7 = (bf16[2,192,768]{2,1,0:T(8,128)(2,1)}, bf16[2,192,768]{2,1,0:T(8,128)(2,1)}, u32[]{:S(2)}, u32[]{:S(2)}) collective-permute-start(bf16[2,192,768]{2,1,0:T(8,128)(2,1)} %pad_maximum_fusion.9), channel_id=1, source_target_pairs={{0,4},{1,5},{2,6},{3,7},{4,0},{5,1},{6,2},{7,3},{8,12},{9,13},{10,... | collective-permute-start | bytes 1769480 | tf_op jit(solution)/shard_map/ppermute | solution.py:41
  110.5 5.4 %collective-permute-start.10 = (bf16[8,240,768]{2,1,0:T(8,128)(2,1)S(1)}, bf16[8,240,768]{2,1,0:T(8,128)(2,1)S(1)}, u32[]{:S(2)}, u32[]{:S(2)}) collective-permute-start(bf16[8,240,768]{2,1,0:T(8,128)(2,1)S(1)} %pad_maximum_fusion.near.near_up), channel_id=1, source_target_pairs={{0,1},{1,0},{2,3},{3,2},{4,5},{5,4},{6,7},{7,6},{8,9},{9,8},{10,11... | collective-permute-start | bytes 8847368 | tf_op jit(solution)/shard_map/ppermute | solution.py:41
  112.7 28.7 %collective-permute-start.9 = (bf16[4,192,768]{2,1,0:T(8,128)(2,1)S(1)}, bf16[4,192,768]{2,1,0:T(8,128)(2,1)S(1)}, u32[]{:S(2)}, u32[]{:S(2)}) collective-permute-start(bf16[4,192,768]{2,1,0:T(8,128)(2,1)S(1)} %pad_maximum_fusion.4), channel_id=1, source_target_pairs={{0,2},{1,3},{2,0},{3,1},{4,6},{5,7},{6,4},{7,5},{8,10},{9,11},{10,... | collective-permute-start | bytes 3538952 | tf_op jit(solution)/shard_map/ppermute | solution.py:41
  165.3 5.5 %collective-permute-start.13 = (bf16[1,32,768]{2,1,0:T(8,128)(2,1)S(1)}, bf16[1,32,768]{2,1,0:T(8,128)(2,1)S(1)}, u32[]{:S(2)}, u32[]{:S(2)}) collective-permute-start(bf16[1,32,768]{2,1,0:T(8,128)(2,1)S(1)} %bitcast.160), channel_id=1, source_target_pairs={{0,8},{1,9},{2,10},{3,11},{4,12},{5,13},{6,14},{7,15},{8,0},{9,1},... | collective-permute-start | bytes 147464 | tf_op jit(solution)/shard_map/ppermute | solution.py:41
  175.5 5.7 %collective-permute-start.15 = (bf16[4,32,768]{2,1,0:T(8,128)(2,1)S(1)}, bf16[4,32,768]{2,1,0:T(8,128)(2,1)S(1)}, u32[]{:S(2)}, u32[]{:S(2)}) collective-permute-start(bf16[4,32,768]{2,1,0:T(8,128)(2,1)S(1)} %pad_maximum_fusion.13), channel_id=1, source_target_pairs={{0,2},{1,3},{2,0},{3,1},{4,6},{5,7},{6,4},{7,5},{8,10},{9,11},{10,... | collective-permute-start | bytes 589832 | tf_op jit(solution)/shard_map/ppermute | solution.py:41
  204.7 36.8 %collective-permute-start.18 = (bf16[4,192,768]{2,1,0:T(8,128)(2,1)S(1)}, bf16[4,192,768]{2,1,0:T(8,128)(2,1)S(1)}, u32[]{:S(2)}, u32[]{:S(2)}) collective-permute-start(bf16[4,192,768]{2,1,0:T(8,128)(2,1)S(1)} %get-tuple-element.243), channel_id=1, source_target_pairs={{0,2},{1,3},{2,0},{3,1},{4,6},{5,7},{6,4},{7,5},{8,10},{9,11},{10,... | collective-permute-start | bytes 3538952 | tf_op jit(solution)/shard_map/ppermute | solution.py:41
  241.5 21.2 %collective-permute-start.20 = (bf16[8,192,768]{2,1,0:T(8,128)(2,1)}, bf16[8,192,768]{2,1,0:T(8,128)(2,1)S(1)}, u32[]{:S(2)}, u32[]{:S(2)}) collective-permute-start(bf16[8,192,768]{2,1,0:T(8,128)(2,1)} %get-tuple-element.150), channel_id=1, source_target_pairs={{0,1},{1,0},{2,3},{3,2},{4,5},{5,4},{6,7},{7,6},{8,9},{9,8},{10,11... | collective-permute-start | bytes 7077896 | tf_op jit(solution)/shard_map/ppermute | solution.py:41
  241.9 20.7 %collective-permute-start.19 = (bf16[2,192,768]{2,1,0:T(8,128)(2,1)S(1)}, bf16[2,192,768]{2,1,0:T(8,128)(2,1)S(1)}, u32[]{:S(2)}, u32[]{:S(2)}) collective-permute-start(bf16[2,192,768]{2,1,0:T(8,128)(2,1)S(1)} %get-tuple-element.250), channel_id=1, source_target_pairs={{0,4},{1,5},{2,6},{3,7},{4,0},{5,1},{6,2},{7,3},{8,12},{9,13},{10,... | collective-permute-start | bytes 1769480 | tf_op jit(solution)/shard_map/ppermute | solution.py:41
  264.3 28.4 %collective-permute-start.22 = (bf16[4,192,768]{2,1,0:T(8,128)(2,1)S(1)}, bf16[4,192,768]{2,1,0:T(8,128)(2,1)S(1)}, u32[]{:S(2)}, u32[]{:S(2)}) collective-permute-start(bf16[4,192,768]{2,1,0:T(8,128)(2,1)S(1)} %get-tuple-element.241), channel_id=1, source_target_pairs={{0,2},{1,3},{2,0},{3,1},{4,6},{5,7},{6,4},{7,5},{8,10},{9,11},{10,... | collective-permute-start | bytes 3538952 | tf_op jit(solution)/shard_map/ppermute | solution.py:41
  265.2 27.6 %collective-permute-start.23 = (bf16[8,96,768]{2,1,0:T(8,128)(2,1)S(1)}, bf16[8,96,768]{2,1,0:T(8,128)(2,1)S(1)}, u32[]{:S(2)}, u32[]{:S(2)}) collective-permute-start(bf16[8,96,768]{2,1,0:T(8,128)(2,1)S(1)} %pad_maximum_fusion.5), channel_id=1, source_target_pairs={{0,1},{1,0},{2,3},{3,2},{4,5},{5,4},{6,7},{7,6},{8,9},{9,8},{10,11... | collective-permute-start | bytes 3538952 | tf_op jit(solution)/shard_map/ppermute | solution.py:41
  266.1 19.3 %collective-permute-start.21 = (bf16[1,192,768]{2,1,0:T(8,128)(2,1)S(1)}, bf16[1,192,768]{2,1,0:T(8,128)(2,1)S(1)}, u32[]{:S(2)}, u32[]{:S(2)}) collective-permute-start(bf16[1,192,768]{2,1,0:T(8,128)(2,1)S(1)} %add_convert_fusion.19), channel_id=1, source_target_pairs={{0,8},{1,9},{2,10},{3,11},{4,12},{5,13},{6,14},{7,15},{8,0},{9,1},... | collective-permute-start | bytes 884744 | tf_op jit(solution)/shard_map/ppermute | solution.py:41
  294.1 20.2 %collective-permute-start.24 = (bf16[2,192,768]{2,1,0:T(8,128)(2,1)}, bf16[2,192,768]{2,1,0:T(8,128)(2,1)}, u32[]{:S(2)}, u32[]{:S(2)}) collective-permute-start(bf16[2,192,768]{2,1,0:T(8,128)(2,1)} %get-tuple-element.246), channel_id=1, source_target_pairs={{0,4},{1,5},{2,6},{3,7},{4,0},{5,1},{6,2},{7,3},{8,12},{9,13},{10,... | collective-permute-start | bytes 1769480 | tf_op jit(solution)/shard_map/ppermute | solution.py:41
  295.5 18.8 %collective-permute-start.25 = (bf16[4,96,768]{2,1,0:T(8,128)(2,1)}, bf16[4,96,768]{2,1,0:T(8,128)(2,1)}, u32[]{:S(2)}, u32[]{:S(2)}) collective-permute-start(bf16[4,96,768]{2,1,0:T(8,128)(2,1)} %get-tuple-element.248), channel_id=1, source_target_pairs={{0,2},{1,3},{2,0},{3,1},{4,6},{5,7},{6,4},{7,5},{8,10},{9,11},{10,... | collective-permute-start | bytes 1769480 | tf_op jit(solution)/shard_map/ppermute | solution.py:41
  296.3 18.0 %collective-permute-start.26 = (bf16[8,48,768]{2,1,0:T(8,128)(2,1)S(1)}, bf16[8,48,768]{2,1,0:T(8,128)(2,1)}, u32[]{:S(2)}, u32[]{:S(2)}) collective-permute-start(bf16[8,48,768]{2,1,0:T(8,128)(2,1)S(1)} %get-tuple-element.168), channel_id=1, source_target_pairs={{0,1},{1,0},{2,3},{3,2},{4,5},{5,4},{6,7},{7,6},{8,9},{9,8},{10,11... | collective-permute-start | bytes 1769480 | tf_op jit(solution)/shard_map/ppermute | solution.py:41
  315.4 17.2 %collective-permute-start.27 = (bf16[1,192,768]{2,1,0:T(8,128)(2,1)S(1)}, bf16[1,192,768]{2,1,0:T(8,128)(2,1)S(1)}, u32[]{:S(2)}, u32[]{:S(2)}) collective-permute-start(bf16[1,192,768]{2,1,0:T(8,128)(2,1)S(1)} %add_convert_fusion.17), channel_id=1, source_target_pairs={{0,8},{1,9},{2,10},{3,11},{4,12},{5,13},{6,14},{7,15},{8,0},{9,1},... | collective-permute-start | bytes 884744 | tf_op jit(solution)/shard_map/ppermute | solution.py:41
  318.6 16.4 %collective-permute-start.30 = (bf16[8,64,768]{2,1,0:T(8,128)(2,1)S(1)}, bf16[8,64,768]{2,1,0:T(8,128)(2,1)S(1)}, u32[]{:S(2)}, u32[]{:S(2)}) collective-permute-start(bf16[8,64,768]{2,1,0:T(8,128)(2,1)S(1)} %pad_maximum_fusion.6), channel_id=1, source_target_pairs={{0,1},{1,0},{2,3},{3,2},{4,5},{5,4},{6,7},{7,6},{8,9},{9,8},{10,11... | collective-permute-start | bytes 2359304 | tf_op jit(solution)/shard_map/ppermute | solution.py:41
  320.3 14.6 %collective-permute-start.28 = (bf16[2,96,768]{2,1,0:T(8,128)(2,1)S(1)}, bf16[2,96,768]{2,1,0:T(8,128)(2,1)S(1)}, u32[]{:S(2)}, u32[]{:S(2)}) collective-permute-start(bf16[2,96,768]{2,1,0:T(8,128)(2,1)S(1)} %get-tuple-element.255), channel_id=1, source_target_pairs={{0,4},{1,5},{2,6},{3,7},{4,0},{5,1},{6,2},{7,3},{8,12},{9,13},{10,... | collective-permute-start | bytes 884744 | tf_op jit(solution)/shard_map/ppermute | solution.py:41
  321.9 13.1 %collective-permute-start.29 = (bf16[4,48,768]{2,1,0:T(8,128)(2,1)S(1)}, bf16[4,48,768]{2,1,0:T(8,128)(2,1)S(1)}, u32[]{:S(2)}, u32[]{:S(2)}) collective-permute-start(bf16[4,48,768]{2,1,0:T(8,128)(2,1)S(1)} %get-tuple-element.254), channel_id=1, source_target_pairs={{0,2},{1,3},{2,0},{3,1},{4,6},{5,7},{6,4},{7,5},{8,10},{9,11},{10,... | collective-permute-start | bytes 884744 | tf_op jit(solution)/shard_map/ppermute | solution.py:41
  335.0 8.5 %collective-permute-start.31 = (bf16[1,96,768]{2,1,0:T(8,128)(2,1)S(1)}, bf16[1,96,768]{2,1,0:T(8,128)(2,1)S(1)}, u32[]{:S(2)}, u32[]{:S(2)}) collective-permute-start(bf16[1,96,768]{2,1,0:T(8,128)(2,1)S(1)} %add_convert_fusion.24), channel_id=1, source_target_pairs={{0,8},{1,9},{2,10},{3,11},{4,12},{5,13},{6,14},{7,15},{8,0},{9,1},... | collective-permute-start | bytes 442376 | tf_op jit(solution)/shard_map/ppermute | solution.py:41
  335.3 10.6 %collective-permute-start.33 = (bf16[4,64,768]{2,1,0:T(8,128)(2,1)S(1)}, bf16[4,64,768]{2,1,0:T(8,128)(2,1)S(1)}, u32[]{:S(2)}, u32[]{:S(2)}) collective-permute-start(bf16[4,64,768]{2,1,0:T(8,128)(2,1)S(1)} %get-tuple-element.252), channel_id=1, source_target_pairs={{0,2},{1,3},{2,0},{3,1},{4,6},{5,7},{6,4},{7,5},{8,10},{9,11},{10,... | collective-permute-start | bytes 1179656 | tf_op jit(solution)/shard_map/ppermute | solution.py:41
  336.6 8.3 %collective-permute-start.32 = (bf16[2,48,768]{2,1,0:T(8,128)(2,1)S(1)}, bf16[2,48,768]{2,1,0:T(8,128)(2,1)S(1)}, u32[]{:S(2)}, u32[]{:S(2)}) collective-permute-start(bf16[2,48,768]{2,1,0:T(8,128)(2,1)S(1)} %get-tuple-element.260), channel_id=1, source_target_pairs={{0,4},{1,5},{2,6},{3,7},{4,0},{5,1},{6,2},{7,3},{8,12},{9,13},{10,... | collective-permute-start | bytes 442376 | tf_op jit(solution)/shard_map/ppermute | solution.py:41
  346.7 7.0 %collective-permute-start.35 = (bf16[2,64,768]{2,1,0:T(8,128)(2,1)S(1)}, bf16[2,64,768]{2,1,0:T(8,128)(2,1)S(1)}, u32[]{:S(2)}, u32[]{:S(2)}) collective-permute-start(bf16[2,64,768]{2,1,0:T(8,128)(2,1)S(1)} %get-tuple-element.258), channel_id=1, source_target_pairs={{0,4},{1,5},{2,6},{3,7},{4,0},{5,1},{6,2},{7,3},{8,12},{9,13},{10,... | collective-permute-start | bytes 589832 | tf_op jit(solution)/shard_map/ppermute | solution.py:41
  347.9 5.6 %collective-permute-start.34 = (bf16[1,48,768]{2,1,0:T(8,128)(2,1)S(1)}, bf16[1,48,768]{2,1,0:T(8,128)(2,1)S(1)}, u32[]{:S(2)}, u32[]{:S(2)}) collective-permute-start(bf16[1,48,768]{2,1,0:T(8,128)(2,1)S(1)} %add_convert_fusion.28), channel_id=1, source_target_pairs={{0,8},{1,9},{2,10},{3,11},{4,12},{5,13},{6,14},{7,15},{8,0},{9,1},... | collective-permute-start | bytes 221192 | tf_op jit(solution)/shard_map/ppermute | solution.py:41
  354.7 5.6 %collective-permute-start.36 = (bf16[1,64,768]{2,1,0:T(8,128)(2,1)S(1)}, bf16[1,64,768]{2,1,0:T(8,128)(2,1)S(1)}, u32[]{:S(2)}, u32[]{:S(2)}) collective-permute-start(bf16[1,64,768]{2,1,0:T(8,128)(2,1)S(1)} %add_convert_fusion.26), channel_id=1, source_target_pairs={{0,8},{1,9},{2,10},{3,11},{4,12},{5,13},{6,14},{7,15},{8,0},{9,1},... | collective-permute-start | bytes 294920 | tf_op jit(solution)/shard_map/ppermute | solution.py:41
  (73 other events, 680.1 us)
